TPU v7x, 32 devices: a whole 2x2x4 slice. The times are simulated.
32 devices in a mesh: row: 8 (over z, x), col: 4 (over y, core).
Axes of the slice: x: 2, y: 2, z: 4, core: 2. Of those that a mesh axis runs over, the one named last changes fastest.
Arguments:
- block_values: bfloat16 [8, 4, 256, 128, 128], P('row', 'col')
- block_rows: int32 [8, 4, 256], P('row', 'col'), may hold values from -1 to 511, as said below
- block_cols: int32 [8, 4, 256], P('row', 'col'), may hold values from -1 to 511, as said below
- cost_vec: float32 [262144], P('col')
- demand: float32 [524288], P('row')
- lower: float32 [262144], P('col'), may hold values from -1.5 to -0.2
- upper: float32 [262144], P('col'), may hold values from 0.2 to 1.5
- bound_kind: int32 [262144], P('col'), may hold values from 0 to 3
- primal_start: float32 [262144], P('col'), may hold values from -4 to 4
- dual_start: float32 [524288], P('row'), may hold values from 0 to 1.5
Outputs:
- primal_out: float32 [262144], P('col')
- dual_out: float32 [524288], P('row')
Inputs may be any that keep to these rules, and one draw needn't show every extreme that they name: A slot's block_rows and block_cols are both -1 exactly when the slot is empty; the live slots of a device come first, a device has at least 128 of them, and in every draw some device has all 256 slots live and some device has empty slots; every block row and every block column of the whole matrix is named by some live slot; a block place may be named by several slots. `block_cols`: as for block_rows.
All inputs are finite; a program needn't handle non-finite values.
Results may differ from a plain program's by a relative error of at most 0.0073.
Values sent between devices are 32-bit elements; how exact they have to be, the bound alone decides.
No kernel may reach another device: no remote copies, remote signals or barrier semaphores. Data moves between devices by JAX's collectives and lax.ppermute only.
A program may use at most 64 MiB of HBM per device.

v0:
```python
import functools

import jax
import jax.numpy as jnp
from jax import lax
from jax.experimental import pallas as pl
from jax.experimental.pallas import tpu as pltpu
from jax.sharding import PartitionSpec as P

SMALL_EPS = 1e-06
STEP_SCALE = 0.3

CHUNKS = 8
FIRST_GROUP = 32
GROUP = 64
AHEAD = 3
ROW_HALVING = 1
QUARTERS = 4
FIRST_VMEM = 44 * 1024 * 1024
BLOCK_VMEM = 20 * 1024 * 1024
SMALL_VMEM = 8 * 1024 * 1024


def bit_of(index, bit):
    return jnp.where((index & bit) != 0, 1, 0)


def row_mask():
    return bit_of(lax.axis_index("col"), ROW_HALVING) * (CHUNKS // 2)


def col_mask():
    return (lax.axis_index("row") & (QUARTERS - 1)) * (CHUNKS // QUARTERS)


def col_place(tile, count, mask):
    return jnp.where(tile < 0, count, tile ^ (mask * (count // CHUNKS)))


def row_place(tile, count, mask):
    return jnp.where(tile < 0, count, tile ^ (mask * (count // CHUNKS)))


def chunk_rows(chunk, size):
    return pl.ds(pl.multiple_of(chunk * size, size), size)


def piece_chunk(pieces, place, size, offset=0):
    per_piece = CHUNKS // len(pieces)
    start = offset + (place % per_piece) * size
    return pieces[place // per_piece], pl.ds(start, size)


def store_pieces(acc, pieces, count):
    size = count // len(pieces)
    for index, piece in enumerate(pieces):
        piece[...] = acc[pl.ds(index * size, size), :]


def add_row(acc, place, term, combine):
    acc[pl.ds(place, 1), :] = combine(acc[pl.ds(place, 1), :], term)


def one_row(ref, tile):
    return ref[pl.ds(jnp.maximum(tile, 0), 1), :]


def tree_of(parts, combine):
    while len(parts) > 1:
        parts = [combine(parts[i], parts[i + 1]) for i in range(0, len(parts), 2)]
    return parts[0]


def tree_sum(parts):
    return tree_of(parts, jnp.add)


def fold_rows(values):
    return jnp.sum(values.reshape(-1, 8, values.shape[-1]), axis=0)


def block_copy(index, values_ref, blocks, arrived):
    part = pl.ds(pl.multiple_of(index * FIRST_GROUP, FIRST_GROUP), FIRST_GROUP)
    return pltpu.make_async_copy(values_ref.at[part], blocks.at[part], arrived.at[index])


def for_slots(ids_ref, visit, finish, group=GROUP, before=None):
    count = ids_ref.shape[0] // 2

    def step(index, carry):
        if before is not None:
            before(index)
        slots = [index * group + inner for inner in range(group)]
        ids = [(ids_ref[slot], ids_ref[count + slot]) for slot in slots]
        terms = visit(slots, ids)
        for (row, col), term in zip(ids, terms):
            finish(row, col, term)
        return carry

    lax.fori_loop(0, count // group, step, 0)


def product_terms(vector_ref, tiles, blocks):
    width = vector_ref.shape[1]
    place = lax.broadcasted_iota(jnp.int32, (8, width), 0)
    terms = []
    for start in range(0, len(tiles), 4):
        rows = [one_row(vector_ref, tile) for tile in tiles[start : start + 4]]
        left = jnp.where(place == 0, rows[0], jnp.where(place == 1, rows[1], 0.0))
        right = jnp.where(place == 2, rows[2], jnp.where(place == 3, rows[3], 0.0))
        quad = blocks[start : start + 4]
        found = jnp.dot(
            jnp.concatenate([left, right], axis=1).astype(jnp.bfloat16),
            jnp.concatenate(
                [jnp.concatenate(quad[:2], axis=1), jnp.concatenate(quad[2:], axis=1)], axis=0
            ),
            preferred_element_type=jnp.float32,
        )
        for index in range(4):
            side = (index % 2) * width
            terms.append(found[index : index + 1, side : side + width])
    return terms


def row_max(values):
    return jnp.max(values, axis=0, keepdims=True)


def packed_max(values):
    folded = jnp.max(values.reshape(-1, 16, values.shape[-1]), axis=0)
    return row_max(folded.astype(jnp.float32))


def first_pass_kernel(count, ids_ref, values_ref, *refs):
    row_out, col_out, blocks = refs[:2], refs[2:6], refs[6]
    arrived, row_acc, col_acc = refs[7:]
    mask, across = col_mask(), row_mask()
    groups = values_ref.shape[0] // FIRST_GROUP
    for index in range(min(AHEAD, groups)):
        block_copy(index, values_ref, blocks, arrived).start()
    for acc in (row_acc, col_acc):
        acc[...] = jnp.zeros_like(acc)

    def before(index):
        block_copy(index, values_ref, blocks, arrived).wait()

        @pl.when(index + AHEAD < groups)
        def _():
            block_copy(index + AHEAD, values_ref, blocks, arrived).start()

    def visit(slots, ids):
        sizes = [jnp.abs(blocks[slot]) for slot in slots]
        return [(packed_max(size.T), packed_max(size)) for size in sizes]

    def finish(row, col, terms):
        add_row(row_acc, row_place(row, count, across), terms[0], jnp.maximum)
        add_row(col_acc, col_place(col, count, mask), terms[1], jnp.maximum)

    for_slots(ids_ref, visit, finish, FIRST_GROUP, before)
    store_pieces(row_acc, row_out, count)
    store_pieces(col_acc, col_out, count)


def first_product_kernel(count, ids_ref, blocks, dual_ref, *refs):
    product_out, turned, product_acc = refs[:4], refs[4], refs[5]
    mask = col_mask()
    product_acc[...] = jnp.zeros_like(product_acc)

    def visit(slots, ids):
        found = [blocks[slot] for slot in slots]
        for slot, block in zip(slots, found):
            turned[slot] = block.T
        return product_terms(dual_ref, [row for row, _ in ids], found)

    def finish(row, col, term):
        add_row(product_acc, col_place(col, count, mask), term, jnp.add)

    for_slots(ids_ref, visit, finish)
    store_pieces(product_acc, product_out, count)


def scaled_peaks(slots, scales, direct, flipped):
    width = direct.shape[-1]
    square = (width, width)
    diagonal = lax.broadcasted_iota(jnp.int32, square, 0) == lax.broadcasted_iota(
        jnp.int32, square, 1
    )
    diagonal = diagonal.astype(jnp.float32).astype(jnp.bfloat16)
    found = []
    for index, (slot, scale) in enumerate(zip(slots, scales)):
        if index % 2:
            scaled = (jnp.abs(flipped[slot]).astype(jnp.float32) * scale).T
        else:
            sizes = jnp.abs(direct[slot])
            high = scale.astype(jnp.bfloat16)
            low = (scale - high.astype(jnp.float32)).astype(jnp.bfloat16)
            scaled = jnp.dot(
                jnp.concatenate([diagonal * high, diagonal * low], axis=1),
                jnp.concatenate([sizes, sizes], axis=0),
                preferred_element_type=jnp.float32,
            )
        found.append(row_max(scaled))
    return found


def second_cols_kernel(count, ids_ref, blocks, turned, *refs):
    row_in, col_out, row_scale, col_acc = refs[:2], refs[2:6], refs[6], refs[7]
    mask, across = col_mask(), row_mask()
    size = count // CHUNKS
    col_acc[...] = jnp.zeros_like(col_acc)
    for place in range(CHUNKS):
        piece, part = piece_chunk(row_in, place, size)
        row_scale[chunk_rows(place ^ across, size), :] = lax.rsqrt(piece[part, :] + SMALL_EPS)

    def visit(slots, ids):
        scales = [one_row(row_scale, row) for row, _ in ids]
        return scaled_peaks(slots, scales, blocks, turned)

    def finish(row, col, term):
        add_row(col_acc, col_place(col, count, mask), term, jnp.maximum)

    for_slots(ids_ref, visit, finish)
    store_pieces(col_acc, col_out, count)


def second_rows_kernel(count, ids_ref, blocks, turned, *refs):
    col_in, row_out, col_scale, row_acc = refs[:4], refs[4:6], refs[6], refs[7]
    mask, across = col_mask(), row_mask()
    size = count // CHUNKS
    row_acc[...] = jnp.zeros_like(row_acc)
    for place in range(CHUNKS):
        piece, part = piece_chunk(col_in, place, size)
        col_scale[chunk_rows(place ^ mask, size), :] = lax.rsqrt(piece[part, :] + SMALL_EPS)

    def visit(slots, ids):
        scales = [one_row(col_scale, col) for _, col in ids]
        return scaled_peaks(slots, scales, turned, blocks)

    def finish(row, col, term):
        add_row(row_acc, row_place(row, count, across), term, jnp.maximum)

    for_slots(ids_ref, visit, finish)
    store_pieces(row_acc, row_out, count)


def next_scale(scale, piece, inside):
    return scale * lax.rsqrt(scale * piece[inside, :] + SMALL_EPS)


def row_scale_kernel(count, near, far, scale_ref, vector_ref, new_scale, squares):
    across = row_mask()
    size = count // CHUNKS
    sums = []
    for place in range(CHUNKS):
        part = chunk_rows(place ^ across, size)
        piece, inside = piece_chunk((near, far), place, size)
        scale = next_scale(scale_ref[part, :], piece, inside)
        new_scale[part, :] = scale
        scaled = scale * vector_ref[part, :]
        sums.append(fold_rows(scaled * scaled))
    half = CHUNKS // 2
    squares[...] = tree_sum(sums[:half]) + tree_sum(sums[half:])


def col_scale_kernel(count, *refs):
    pieces, (scale_ref, vector_ref, new_scale, squares) = refs[:4], refs[4:]
    mask = col_mask()
    size = count // CHUNKS
    sums = []
    for place in range(CHUNKS):
        part = chunk_rows(place ^ mask, size)
        piece, inside = piece_chunk(pieces, place, size)
        scale = next_scale(scale_ref[part, :], piece, inside)
        new_scale[part, :] = scale
        scaled = scale * vector_ref[part, :]
        sums.append(fold_rows(scaled * scaled))
    squares[...] = tree_sum(sums)


def norm_ratio(cost_squares, demand_squares):
    cost_total = jnp.sum(cost_squares[...], keepdims=True)
    demand_total = jnp.sum(demand_squares[...], keepdims=True)
    return jnp.sqrt(cost_total + SMALL_EPS) / jnp.sqrt(demand_total + SMALL_EPS)


def forward_kernel(count, first, last, ids_ref, turned, *refs):
    product, refs = refs[:4], refs[4:]
    scale_ref, cost_ref, low_ref, high_ref, kind_ref, primal_ref = refs[:6]
    cost_squares, demand_squares, primal_out = refs[6:9]
    row_out, refs = refs[9:11], refs[11:]
    shifted, row_acc = refs[:2]
    moved_ref = primal_out
    if last:
        moved_ref, written = refs[2:]
    mask, across = col_mask(), row_mask()
    size = count // CHUNKS
    row_acc[...] = jnp.zeros_like(row_acc)
    primal_step = STEP_SCALE / norm_ratio(cost_squares, demand_squares)
    for place in range(CHUNKS):
        part = chunk_rows(place ^ mask, size)
        behind = product[0].shape[0] - count // QUARTERS
        piece, inside = piece_chunk(product, place, size, behind)
        scale = scale_ref[part, :]
        inverse = 1.0 / scale
        primal = primal_ref[part, :]
        if first:
            primal = primal * inverse
        gradient = scale * piece[inside, :]
        moved = primal - primal_step * (scale * cost_ref[part, :] - gradient)
        kind = kind_ref[part, :]
        moved = jnp.where(
            (kind == 1) | (kind == 3), jnp.maximum(moved, low_ref[part, :] * inverse), moved
        )
        moved = jnp.where(
            (kind == 2) | (kind == 3), jnp.minimum(moved, high_ref[part, :] * inverse), moved
        )
        shifted[part, :] = scale * (2.0 * moved - primal)
        moved_ref[part, :] = scale * moved if last else moved

    if last:
        copy_out = pltpu.make_async_copy(moved_ref, primal_out, written)
        copy_out.start()

    def visit(slots, ids):
        return product_terms(shifted, [col for _, col in ids], [turned[slot] for slot in slots])

    def finish(row, col, term):
        add_row(row_acc, row_place(row, count, across), term, jnp.add)

    for_slots(ids_ref, visit, finish)
    store_pieces(row_acc, row_out, count)
    if last:
        copy_out.wait()


def next_dual(first, image, inside, scale, demand, dual, dual_step):
    if first:
        dual = dual / scale
    row_image = scale * image[inside, :]
    return jnp.maximum(dual + dual_step * (scale * demand - row_image), 0.0)


def transposed_kernel(count, first, ids_ref, blocks, *refs):
    image, refs = refs[:2], refs[2:]
    scale_ref, demand_ref, dual_ref, cost_squares, demand_squares, dual_out = refs[:6]
    product_out, (weights, product_acc) = refs[6:10], refs[10:]
    mask, across = col_mask(), row_mask()
    size = count // CHUNKS
    product_acc[...] = jnp.zeros_like(product_acc)
    dual_step = STEP_SCALE * norm_ratio(cost_squares, demand_squares)
    for place in range(CHUNKS):
        part = chunk_rows(place ^ across, size)
        piece, inside = piece_chunk(image, place, size)
        scale = scale_ref[part, :]
        dual = next_dual(
            first, piece, inside, scale, demand_ref[part, :], dual_ref[part, :], dual_step
        )
        dual_out[part, :] = dual
        weights[part, :] = scale * dual

    def visit(slots, ids):
        return product_terms(weights, [row for row, _ in ids], [blocks[slot] for slot in slots])

    def finish(row, col, term):
        add_row(product_acc, col_place(col, count, mask), term, jnp.add)

    for_slots(ids_ref, visit, finish)
    store_pieces(product_acc, product_out, count)


def last_dual_kernel(count, first, *refs):
    image, refs = refs[:2], refs[2:]
    scale_ref, demand_ref, dual_ref, cost_squares, demand_squares, dual_out = refs
    across = row_mask()
    size = count // CHUNKS
    dual_step = STEP_SCALE * norm_ratio(cost_squares, demand_squares)
    for place in range(CHUNKS):
        part = chunk_rows(place ^ across, size)
        piece, inside = piece_chunk(image, place, size)
        scale = scale_ref[part, :]
        dual = next_dual(
            first, piece, inside, scale, demand_ref[part, :], dual_ref[part, :], dual_step
        )
        dual_out[part, :] = scale * dual


def vectors(*row_counts):
    return [jax.ShapeDtypeStruct((rows, 128), jnp.float32) for rows in row_counts]


def call_plain(kernel, operands, out_shape):
    return pl.pallas_call(
        kernel,
        out_shape=out_shape,
        in_specs=[pl.BlockSpec(memory_space=pltpu.VMEM)] * len(operands),
        out_specs=[pl.BlockSpec(memory_space=pltpu.VMEM)] * len(out_shape),
        compiler_params=pltpu.CompilerParams(vmem_limit_bytes=SMALL_VMEM),
    )(*operands)


def call_blocks(kernel, ids, values, operands, out_shape, scratch, first=False, last=False):
    width = values.shape[1]
    scratch_shapes = [pltpu.VMEM((rows, width), jnp.float32) for rows in scratch]
    if first:
        arrivals = pltpu.SemaphoreType.DMA((values.shape[0] // FIRST_GROUP,))
        scratch_shapes = [arrivals] + scratch_shapes
    out_specs = [pl.BlockSpec(memory_space=pltpu.VMEM)] * len(out_shape)
    if last:
        out_specs[0] = pl.BlockSpec(memory_space=pl.ANY)
        scratch_shapes = scratch_shapes + [
            pltpu.VMEM(out_shape[0].shape, out_shape[0].dtype),
            pltpu.SemaphoreType.DMA,
        ]
    return pl.pallas_call(
        kernel,
        out_shape=out_shape,
        in_specs=[pl.BlockSpec(memory_space=pltpu.SMEM)]
        + [pl.BlockSpec(memory_space=pl.ANY if first else pltpu.VMEM)]
        + [pl.BlockSpec(memory_space=pltpu.VMEM)] * len(operands),
        out_specs=out_specs,
        scratch_shapes=scratch_shapes,
        compiler_params=pltpu.CompilerParams(
            vmem_limit_bytes=FIRST_VMEM if first else BLOCK_VMEM
        ),
        cost_estimate=pl.CostEstimate(
            flops=2 * values.size, bytes_accessed=2 * values.size, transcendentals=0
        ),
    )(ids, values, *operands)


def swap(vector, axis, size, bit):
    return lax.ppermute(vector, axis, [(i, i ^ bit) for i in range(size)])


def after(values, *earlier):
    return lax.optimization_barrier((values, earlier))[0]


def halve_rows(pieces, groups, combine):
    near, far = pieces
    return combine(near, swap(far, "col", groups, ROW_HALVING))


def exchange_rows(near, groups, combine):
    bit = 1
    while bit < groups:
        if bit != ROW_HALVING:
            near = combine(near, swap(near, "col", groups, bit))
        bit *= 2
    return near


def join_rows(near, groups):
    return [near, swap(near, "col", groups, ROW_HALVING)]


def scatter_cols(pieces, groups, combine, tie=None):
    diagonal = swap(pieces[3], "row", groups, 3)
    first, second = pieces[1:3] if tie is None else after((pieces[1], pieces[2]), tie)
    first, second = swap(first, "row", groups, 1), swap(second, "row", groups, 2)
    return tree_of([pieces[0], first, second, diagonal], combine)


def exchange_cols(piece, groups, combine):
    bit = QUARTERS
    while bit < groups:
        piece = combine(piece, swap(piece, "row", groups, bit))
        bit *= 2
    return piece


def gather_cols(piece, groups):
    diagonal = swap(piece, "row", groups, 3)
    return [piece, swap(piece, "row", groups, 1), swap(piece, "row", groups, 2), diagonal]


def sum_rows(vector, groups):
    vector = exchange_cols(vector, groups, jnp.add)
    return [vector] + [swap(vector, "row", groups, mask) for mask in (1, 2, 3)]


def sum_cols(vector, groups):
    parts = [vector] + [swap(vector, "col", groups, mask) for mask in range(1, groups)]
    return tree_sum(parts)


def per_device(
    row_groups,
    col_groups,
    block_values,
    block_rows,
    block_cols,
    cost_vec,
    demand,
    lower,
    upper,
    bound_kind,
    primal_start,
    dual_start,
):
    values = block_values[0, 0]
    width = values.shape[1]
    ids = jnp.concatenate([block_rows[0, 0], block_cols[0, 0]])
    row_length, col_length = demand.shape[0], cost_vec.shape[0]
    cost_vec, demand, lower, upper, bound_kind, primal_start, dual_start = [
        v.reshape(-1, width)
        for v in (cost_vec, demand, lower, upper, bound_kind, primal_start, dual_start)
    ]
    count = demand.shape[0]
    half, quarter, spare = count // 2, count // QUARTERS, count + 8
    row_pieces, col_pieces = vectors(half, half), vectors(*[quarter] * QUARTERS)
    whole = vectors(count)
    squares = vectors(8)

    def over_col(pieces, combine):
        near = exchange_rows(halve_rows(pieces, col_groups, combine), col_groups, combine)
        return join_rows(near, col_groups)

    def over_row(pieces, combine):
        share = scatter_cols(pieces, row_groups, combine)
        return gather_cols(exchange_cols(share, row_groups, combine), row_groups)

    block_shape = jax.ShapeDtypeStruct(values.shape, values.dtype)
    out = call_blocks(
        functools.partial(first_pass_kernel, count),
        ids,
        values,
        [],
        row_pieces + col_pieces + [block_shape],
        [spare] * 2,
        first=True,
    )
    blocks = out[6]
    near = halve_rows(out[:2], col_groups, jnp.maximum)
    *product_pieces, turned = call_blocks(
        functools.partial(first_product_kernel, count),
        ids,
        blocks,
        [after(dual_start, near)],
        col_pieces + [block_shape],
        [spare],
    )
    share = scatter_cols(out[2:6], row_groups, jnp.maximum, near)
    near = exchange_rows(near, col_groups, jnp.maximum)
    product = scatter_cols(after(product_pieces, near), row_groups, jnp.add)
    share = after(exchange_cols(share, row_groups, jnp.maximum), product_pieces)
    row_peaks = join_rows(near, col_groups)
    *col_pieces_2, row_scale = call_blocks(
        functools.partial(second_cols_kernel, count),
        ids,
        blocks,
        [turned] + after(row_peaks, share),
        col_pieces + whole,
        [spare],
    )
    col_peaks = gather_cols(share, row_groups)
    share = scatter_cols(after(col_pieces_2, col_peaks), row_groups, jnp.maximum)
    product = exchange_cols(product, row_groups, jnp.add)
    near, far, col_scale = call_blocks(
        functools.partial(second_rows_kernel, count),
        ids,
        blocks,
        [turned] + col_peaks,
        row_pieces + whole,
        [spare],
    )
    near, far = after((near, far), (share, product))
    share = exchange_cols(share, row_groups, jnp.maximum)
    row_scale, demand_squares = call_plain(
        functools.partial(row_scale_kernel, count),
        over_col([near, far], jnp.maximum) + [row_scale, demand],
        whole + squares,
    )
    demand_parts = sum_rows(demand_squares, row_groups)
    gathered = gather_cols(jnp.concatenate([share, product], axis=0), row_groups)
    col_scale, cost_squares = call_plain(
        functools.partial(col_scale_kernel, count),
        gathered + [col_scale, cost_vec],
        whole + squares,
    )
    cost_squares = sum_cols(after(cost_squares, demand_parts[1]), col_groups)
    norms = [cost_squares, tree_sum(demand_parts)]

    def forward(first, last, product, primal):
        out = call_blocks(
            functools.partial(forward_kernel, count, first, last),
            ids,
            turned,
            product + [col_scale, cost_vec, lower, upper, bound_kind, primal] + norms,
            whole + row_pieces,
            [count, spare],
            last=last,
        )
        return out[0], over_col(out[1:], jnp.add)

    primal, image = forward(True, False, gathered, primal_start)
    out = call_blocks(
        functools.partial(transposed_kernel, count, True),
        ids,
        blocks,
        image + [row_scale, demand, dual_start] + norms,
        whole + col_pieces,
        [count, spare],
    )
    dual, product = out[0], over_row(out[1:], jnp.add)
    primal, image = forward(False, True, product, primal)
    (dual,) = call_plain(
        functools.partial(last_dual_kernel, count, False),
        image + [row_scale, demand, dual] + norms,
        whole,
    )
    return primal.reshape(col_length), dual.reshape(row_length)


def solution(mesh):
    def body(*args):
        return per_device(mesh.shape["row"], mesh.shape["col"], *args)

    return jax.shard_map(
        body,
        mesh=mesh,
        in_specs=(
            P("row", "col", None, None, None),
            P("row", "col", None),
            P("row", "col", None),
            P("col"),
            P("row"),
            P("col"),
            P("col"),
            P("col"),
            P("col"),
            P("row"),
        ),
        out_specs=(P("col"), P("row")),
        check_vma=False,
    )
```

profile of v0, /device:TPU:0, one launch (start us, length us, event | category | flops | bytes accessed | tf_op | source)
XLA Modules:
  0.0 111.8 jit_solution(14941219721118893669)
XLA Ops:
  0.6 0.7 pad_add_fusion.ids_ref
  1.4 5.6 %shard_map.113 = (f32[256,128]{1,0:T(8,128)S(1)}, f32[256,128]{1,0:T(8,128)S(1)}, f32[128,128]{1,0:T(8,128)S(1)}, f32[128,128]{1,0:T(8,128)S(1)}, f32[128,128]{1...) custom-call(s32[512]{0:T(512)S(1)} %pad_add_fusion.ids_ref, bf16[256,128,128]{2,1,0:T(8,128)(2,1)} %bitcast.27), custom_call_target="tpu_custom_call" | custom-call | flops 8388608 | bytes 8388608 | tf_op jit(solution)/shard_map/pallas_call | solution.py:414
  7.0 0.6 collective-permute-start
  7.6 3.6 %collective-permute-start.5 = (f32[128,128]{1,0:T(8,128)S(1)}, f32[128,128]{1,0:T(8,128)S(1)}, u32[]{:S(2)}, u32[]{:S(2)}) collective-permute-start(f32[128,128]{1,0:T(8,128)S(1)} %get-tuple-element.64), channel_id=1, source_target_pairs={{0,12},{4,8},{8,4},{12,0},{16,28},{20,24},{24,20},{28,16},{1,13},{... | collective-permute-start | bytes 196616 | tf_op jit(solution)/shard_map/ppermute | solution.py:432
  11.2 0.5 collective-permute-start.3
  11.7 1.4 %collective-permute-start.4 = (f32[128,128]{1,0:T(8,128)S(1)}, f32[128,128]{1,0:T(8,128)S(1)}, u32[]{:S(2)}, u32[]{:S(2)}) collective-permute-start(f32[128,128]{1,0:T(8,128)S(1)} %get-tuple-element.63), channel_id=1, source_target_pairs={{0,8},{4,12},{8,0},{12,4},{16,24},{20,28},{24,16},{28,20},{1,9},{5... | collective-permute-start | bytes 196616 | tf_op jit(solution)/shard_map/ppermute | solution.py:432
  13.1 1.5 %collective-permute-start.1 = (f32[256,128]{1,0:T(8,128)S(1)}, f32[256,128]{1,0:T(8,128)S(1)}, u32[]{:S(2)}, u32[]{:S(2)}) collective-permute-start(f32[256,128]{1,0:T(8,128)S(1)} %max.36), channel_id=1, source_target_pairs={{0,2},{1,3},{2,0},{3,1},{4,6},{5,7},{6,4},{7,5},{8,10},{9,11},{10,... | collective-permute-start | bytes 393224 | tf_op jit(solution)/shard_map/ppermute | solution.py:432
  14.5 3.0 %shard_map.114 = (f32[128,128]{1,0:T(8,128)S(1)}, f32[128,128]{1,0:T(8,128)S(1)}, f32[128,128]{1,0:T(8,128)S(1)}, f32[128,128]{1,0:T(8,128)S(1)}, bf16[256,128,128]{2,1,0:T(8,128)(2,1)S(1)}) custom-call(s32[512]{0:T(512)S(1)} %pad_add_fusion.ids_ref, bf16[256,128,128]{2,1,0:T(8,128)(2,1)S(1)} %get-tuple-element.54.blocks, f32[512,128]{1,0:T(8,128)S(1)} %bitcast.18), custom_call_target="tpu_custom_call" | custom-call | flops 8388608 | bytes 8388608 | tf_op jit(solution)/shard_map/pallas_call | solution.py:414
  17.6 2.8 %collective-permute-start.6 = (f32[128,128]{1,0:T(8,128)S(1)}, f32[128,128]{1,0:T(8,128)S(1)}, u32[]{:S(2)}, u32[]{:S(2)}) collective-permute-start(f32[128,128]{1,0:T(8,128)S(1)} %maximum_maximum_fusion.1), channel_id=1, source_target_pairs={{0,16},{4,20},{8,24},{12,28},{16,0},{20,4},{24,8},{28,12},{1,17},{... | collective-permute-start | bytes 196616 | tf_op jit(solution)/shard_map/ppermute | solution.py:432
  20.4 0.7 collective-permute-start.14
  21.1 1.6 %collective-permute-start.15 = (f32[128,128]{1,0:T(8,128)S(1)}, f32[128,128]{1,0:T(8,128)S(1)}, u32[]{:S(2)}, u32[]{:S(2)}) collective-permute-start(f32[128,128]{1,0:T(8,128)S(1)} %get-tuple-element.82), channel_id=1, source_target_pairs={{0,8},{4,12},{8,0},{12,4},{16,24},{20,28},{24,16},{28,20},{1,9},{5... | collective-permute-start | bytes 196616 | tf_op jit(solution)/shard_map/ppermute | solution.py:432
  22.7 1.2 %collective-permute-start.16 = (f32[128,128]{1,0:T(8,128)S(1)}, f32[128,128]{1,0:T(8,128)S(1)}, u32[]{:S(2)}, u32[]{:S(2)}) collective-permute-start(f32[128,128]{1,0:T(8,128)S(1)} %get-tuple-element.83), channel_id=1, source_target_pairs={{0,12},{4,8},{8,4},{12,0},{16,28},{20,24},{24,20},{28,16},{1,13},{... | collective-permute-start | bytes 196616 | tf_op jit(solution)/shard_map/ppermute | solution.py:432
  24.0 1.7 %collective-permute-start.9 = (f32[128,128]{1,0:T(8,128)S(1)}, f32[128,128]{1,0:T(8,128)S(1)}, u32[]{:S(2)}, u32[]{:S(2)}) collective-permute-start(f32[128,128]{1,0:T(8,128)S(1)} %max.41.refs_0_), channel_id=1, source_target_pairs={{0,12},{4,8},{8,4},{12,0},{16,28},{20,24},{24,20},{28,16},{1,13},{... | collective-permute-start | bytes 196616 | tf_op jit(solution)/shard_map/ppermute | solution.py:432
  25.7 0.4 collective-permute-start.8
  26.2 1.5 %collective-permute-start.7 = (f32[128,128]{1,0:T(8,128)S(1)}, f32[128,128]{1,0:T(8,128)S(1)}, u32[]{:S(2)}, u32[]{:S(2)}) collective-permute-start(f32[128,128]{1,0:T(8,128)S(1)} %max.41.refs_0_), channel_id=1, source_target_pairs={{0,4},{4,0},{8,12},{12,8},{16,20},{20,16},{24,28},{28,24},{1,5},{5... | collective-permute-start | bytes 196616 | tf_op jit(solution)/shard_map/ppermute | solution.py:432
  27.9 1.9 %collective-permute-start.17 = (f32[128,128]{1,0:T(8,128)S(1)}, f32[128,128]{1,0:T(8,128)S(1)}, u32[]{:S(2)}, u32[]{:S(2)}) collective-permute-start(f32[128,128]{1,0:T(8,128)S(1)} %add_add_fusion.1), channel_id=1, source_target_pairs={{0,16},{4,20},{8,24},{12,28},{16,0},{20,4},{24,8},{28,12},{1,17},{... | collective-permute-start | bytes 196616 | tf_op jit(solution)/shard_map/ppermute | solution.py:432
  29.8 4.1 %shard_map.115 = (f32[128,128]{1,0:T(8,128)S(1)}, f32[128,128]{1,0:T(8,128)S(1)}, f32[128,128]{1,0:T(8,128)S(1)}, f32[128,128]{1,0:T(8,128)S(1)}, f32[512,128]{1,0:T(8,128)S(1)}) custom-call(s32[512]{0:T(512)S(1)} %pad_add_fusion.ids_ref, bf16[256,128,128]{2,1,0:T(8,128)(2,1)S(1)} %get-tuple-element.54.blocks, ...), custom_call_target="tpu_custom_call" | custom-call | flops 8388608 | bytes 8388608 | tf_op jit(solution)/shard_map/pallas_call | solution.py:414
  34.0 0.8 collective-permute-start.10
  34.8 1.6 %collective-permute-start.11 = (f32[128,128]{1,0:T(8,128)S(1)}, f32[128,128]{1,0:T(8,128)S(1)}, u32[]{:S(2)}, u32[]{:S(2)}) collective-permute-start(f32[128,128]{1,0:T(8,128)S(1)} %get-tuple-element.78), channel_id=1, source_target_pairs={{0,8},{4,12},{8,0},{12,4},{16,24},{20,28},{24,16},{28,20},{1,9},{5... | collective-permute-start | bytes 196616 | tf_op jit(solution)/shard_map/ppermute | solution.py:432
  36.4 1.1 %collective-permute-start.12 = (f32[128,128]{1,0:T(8,128)S(1)}, f32[128,128]{1,0:T(8,128)S(1)}, u32[]{:S(2)}, u32[]{:S(2)}) collective-permute-start(f32[128,128]{1,0:T(8,128)S(1)} %get-tuple-element.79), channel_id=1, source_target_pairs={{0,12},{4,8},{8,4},{12,0},{16,28},{20,24},{24,20},{28,16},{1,13},{... | collective-permute-start | bytes 196616 | tf_op jit(solution)/shard_map/ppermute | solution.py:432
  37.5 4.1 %shard_map.116 = (f32[256,128]{1,0:T(8,128)S(1)}, f32[256,128]{1,0:T(8,128)S(1)}, f32[512,128]{1,0:T(8,128)S(1)}) custom-call(s32[512]{0:T(512)S(1)} %pad_add_fusion.ids_ref, bf16[256,128,128]{2,1,0:T(8,128)(2,1)S(1)} %get-tuple-element.54.blocks, bf16[256,128,128]{2,1,0:T(8,128)(2,1)S(1)} %get-tuple-element.58.turned, f32[128,128]{1,0:T(8,128)S(1)} %max.41.refs_0_, ...), custom_call_target="tpu_custom_call" | custom-call | flops 8388608 | bytes 8388608 | tf_op jit(solution)/shard_map/pallas_call | solution.py:414
  41.8 1.3 %collective-permute-done.21 = f32[256,128]{1,0:T(8,128)S(1)} collective-permute-done((f32[256,128]{1,0:T(8,128)S(1)}, f32[256,128]{1,0:T(8,128)S(1)}, u32[]{:S(2)}, u32[]{:S(2)}) %collective-permute-start.21) | collective-permute-done | bytes 131104 | tf_op jit(solution)/shard_map/ppermute | solution.py:432
  43.1 0.6 collective-permute-start.22
  43.8 1.1 collective-permute-start.13
  44.8 4.9 %collective-permute-done.13 = f32[128,128]{1,0:T(8,128)S(1)} collective-permute-done((f32[128,128]{1,0:T(8,128)S(1)}, f32[128,128]{1,0:T(8,128)S(1)}, u32[]{:S(2)}, u32[]{:S(2)}) %collective-permute-start.13) | collective-permute-done | bytes 65568 | tf_op jit(solution)/shard_map/ppermute | solution.py:432
  49.9 1.0 collective-permute-start.20
  50.9 1.8 %collective-permute-start.19 = (f32[256,128]{1,0:T(8,128)S(1)}, f32[256,128]{1,0:T(8,128)S(1)}, u32[]{:S(2)}, u32[]{:S(2)}) collective-permute-start(f32[256,128]{1,0:T(8,128)S(1)} %pad_maximum_fusion.refs_0_), channel_id=1, source_target_pairs={{0,8},{4,12},{8,0},{12,4},{16,24},{20,28},{24,16},{28,20},{1,9},{5... | collective-permute-start | bytes 393224 | tf_op jit(solution)/shard_map/ppermute | solution.py:432
  52.7 0.7 collective-permute-start.18
  53.5 0.3 collective-permute-start.24
  53.9 4.4 %collective-permute-done.24 = f32[8,128]{1,0:T(8,128)S(1)} collective-permute-done((f32[8,128]{1,0:T(8,128)S(1)}, f32[8,128]{1,0:T(8,128)S(1)}, u32[]{:S(2)}, u32[]{:S(2)}) %collective-permute-start.24) | collective-permute-done | bytes 4128 | tf_op jit(solution)/shard_map/ppermute | solution.py:432
  58.2 1.3 %collective-permute-start.25 = (f32[8,128]{1,0:T(8,128)S(1)}, f32[8,128]{1,0:T(8,128)S(1)}, u32[]{:S(2)}, u32[]{:S(2)}) collective-permute-start(f32[8,128]{1,0:T(8,128)S(1)} %add.61), channel_id=1, source_target_pairs={{0,4},{4,0},{8,12},{12,8},{16,20},{20,16},{24,28},{28,24},{1,5},{5... | collective-permute-start | bytes 12296 | tf_op jit(solution)/shard_map/ppermute | solution.py:432
  59.5 1.0 collective-permute-start.30
  60.5 1.2 %collective-permute-start.29 = (f32[8,128]{1,0:T(8,128)S(1)}, f32[8,128]{1,0:T(8,128)S(1)}, u32[]{:S(2)}, u32[]{:S(2)}) collective-permute-start(f32[8,128]{1,0:T(8,128)S(1)} %add.61), channel_id=1, source_target_pairs={{0,8},{4,12},{8,0},{12,4},{16,24},{20,28},{24,16},{28,20},{1,9},{5... | collective-permute-start | bytes 12296 | tf_op jit(solution)/shard_map/ppermute | solution.py:432
  61.9 1.6 %collective-permute-start.27 = (f32[8,128]{1,0:T(8,128)S(1)}, f32[8,128]{1,0:T(8,128)S(1)}, u32[]{:S(2)}, u32[]{:S(2)}) collective-permute-start(f32[8,128]{1,0:T(8,128)S(1)} %get-tuple-element.93), channel_id=1, source_target_pairs={{0,2},{1,3},{2,0},{3,1},{4,6},{5,7},{6,4},{7,5},{8,10},{9,11},{10,... | collective-permute-start | bytes 12296 | tf_op jit(solution)/shard_map/ppermute | solution.py:432
  63.5 0.3 collective-permute-start.26
  63.8 0.2 collective-permute-done.30
  64.1 0.8 collective-permute-done.28
  64.9 0.7 collective-permute-done.27
  65.6 2.8 %shard_map.119 = (f32[512,128]{1,0:T(8,128)S(1)}, f32[256,128]{1,0:T(8,128)S(1)}, f32[256,128]{1,0:T(8,128)S(1)}) custom-call(s32[512]{0:T(512)S(1)} %pad_add_fusion.ids_ref, bf16[256,128,128]{2,1,0:T(8,128)(2,1)S(1)} %get-tuple-element.58.turned, f32[256,128]{1,0:T(8,128)S(1)} %pad_maximum_fusion.refs_0_, f32[256,128]{1,0:T(8,128)S(1)} %collective-permute-done.18.refs_1_, ...), custom_call_target="tpu_custom_call" | custom-call | flops 8388608 | bytes 8388608 | tf_op jit(solution)/shard_map/pallas_call | solution.py:414
  68.4 0.6 collective-permute-start.31
  69.0 1.0 collective-permute-done.31
  70.0 1.6 %collective-permute-start.32 = (f32[256,128]{1,0:T(8,128)S(1)}, f32[256,128]{1,0:T(8,128)S(1)}, u32[]{:S(2)}, u32[]{:S(2)}) collective-permute-start(f32[256,128]{1,0:T(8,128)S(1)} %add.68), channel_id=1, source_target_pairs={{0,2},{1,3},{2,0},{3,1},{4,6},{5,7},{6,4},{7,5},{8,10},{9,11},{10,... | collective-permute-start | bytes 393224 | tf_op jit(solution)/shard_map/ppermute | solution.py:432
  71.6 4.3 %collective-permute-done.32 = f32[256,128]{1,0:T(8,128)S(1)} collective-permute-done((f32[256,128]{1,0:T(8,128)S(1)}, f32[256,128]{1,0:T(8,128)S(1)}, u32[]{:S(2)}, u32[]{:S(2)}) %collective-permute-start.32) | collective-permute-done | bytes 131104 | tf_op jit(solution)/shard_map/ppermute | solution.py:432
  75.9 1.3 %collective-permute-done.33.refs_1_ = f32[256,128]{1,0:T(8,128)S(1)} collective-permute-done((f32[256,128]{1,0:T(8,128)S(1)}, f32[256,128]{1,0:T(8,128)S(1)}, u32[]{:S(2)}, u32[]{:S(2)}) %collective-permute-start.33) | collective-permute-done | bytes 131104 | tf_op jit(solution)/shard_map/ppermute | solution.py:432
  77.3 2.6 %shard_map.120 = (f32[512,128]{1,0:T(8,128)S(1)}, f32[128,128]{1,0:T(8,128)S(1)}, f32[128,128]{1,0:T(8,128)S(1)}, f32[128,128]{1,0:T(8,128)S(1)}, f32[128,128]{1,0:T(8,128)S(1)}) custom-call(s32[512]{0:T(512)S(1)} %pad_add_fusion.ids_ref, bf16[256,128,128]{2,1,0:T(8,128)(2,1)S(1)} %get-tuple-element.54.blocks, f32[256,128]{1,0:T(8,128)S(1)} %add.69.refs_0_, ...), custom_call_target="tpu_custom_call" | custom-call | flops 8388608 | bytes 8388608 | tf_op jit(solution)/shard_map/pallas_call | solution.py:414
  79.9 1.3 %collective-permute-start.34 = (f32[128,128]{1,0:T(8,128)S(1)}, f32[128,128]{1,0:T(8,128)S(1)}, u32[]{:S(2)}, u32[]{:S(2)}) collective-permute-start(f32[128,128]{1,0:T(8,128)S(1)} %get-tuple-element.98), channel_id=1, source_target_pairs={{0,4},{4,0},{8,12},{12,8},{16,20},{20,16},{24,28},{28,24},{1,5},{5... | collective-permute-start | bytes 196616 | tf_op jit(solution)/shard_map/ppermute | solution.py:432
  81.2 1.2 %collective-permute-start.35 = (f32[128,128]{1,0:T(8,128)S(1)}, f32[128,128]{1,0:T(8,128)S(1)}, u32[]{:S(2)}, u32[]{:S(2)}) collective-permute-start(f32[128,128]{1,0:T(8,128)S(1)} %get-tuple-element.99), channel_id=1, source_target_pairs={{0,8},{4,12},{8,0},{12,4},{16,24},{20,28},{24,16},{28,20},{1,9},{5... | collective-permute-start | bytes 196616 | tf_op jit(solution)/shard_map/ppermute | solution.py:432
  82.4 1.0 collective-permute-start.36
  83.5 0.8 collective-permute-done.34
  84.3 1.5 %collective-permute-done.35 = f32[128,128]{1,0:T(8,128)S(1)} collective-permute-done((f32[128,128]{1,0:T(8,128)S(1)}, f32[128,128]{1,0:T(8,128)S(1)}, u32[]{:S(2)}, u32[]{:S(2)}) %collective-permute-start.35) | collective-permute-done | bytes 65568 | tf_op jit(solution)/shard_map/ppermute | solution.py:432
  85.8 1.8 %collective-permute-done.36 = f32[128,128]{1,0:T(8,128)S(1)} collective-permute-done((f32[128,128]{1,0:T(8,128)S(1)}, f32[128,128]{1,0:T(8,128)S(1)}, u32[]{:S(2)}, u32[]{:S(2)}) %collective-permute-start.36) | collective-permute-done | bytes 65568 | tf_op jit(solution)/shard_map/ppermute | solution.py:432
  87.6 1.5 %collective-permute-start.37 = (f32[128,128]{1,0:T(8,128)S(1)}, f32[128,128]{1,0:T(8,128)S(1)}, u32[]{:S(2)}, u32[]{:S(2)}) collective-permute-start(f32[128,128]{1,0:T(8,128)S(1)} %add_add_fusion), channel_id=1, source_target_pairs={{0,16},{4,20},{8,24},{12,28},{16,0},{20,4},{24,8},{28,12},{1,17},{... | collective-permute-start | bytes 196616 | tf_op jit(solution)/shard_map/ppermute | solution.py:432
  89.1 4.5 %collective-permute-done.37 = f32[128,128]{1,0:T(8,128)S(1)} collective-permute-done((f32[128,128]{1,0:T(8,128)S(1)}, f32[128,128]{1,0:T(8,128)S(1)}, u32[]{:S(2)}, u32[]{:S(2)}) %collective-permute-start.37) | collective-permute-done | bytes 65568 | tf_op jit(solution)/shard_map/ppermute | solution.py:432
  93.7 0.5 collective-permute-start.40
  94.2 0.6 collective-permute-start.39
  94.7 2.5 %collective-permute-start.38 = (f32[128,128]{1,0:T(8,128)S(1)}, f32[128,128]{1,0:T(8,128)S(1)}, u32[]{:S(2)}, u32[]{:S(2)}) collective-permute-start(f32[128,128]{1,0:T(8,128)S(1)} %add.73.refs_0_), channel_id=1, source_target_pairs={{0,4},{4,0},{8,12},{12,8},{16,20},{20,16},{24,28},{28,24},{1,5},{5... | collective-permute-start | bytes 196616 | tf_op jit(solution)/shard_map/ppermute | solution.py:432
  97.2 1.7 %collective-permute-done.40.refs_3_ = f32[128,128]{1,0:T(8,128)S(1)} collective-permute-done((f32[128,128]{1,0:T(8,128)S(1)}, f32[128,128]{1,0:T(8,128)S(1)}, u32[]{:S(2)}, u32[]{:S(2)}) %collective-permute-start.40) | collective-permute-done | bytes 65568 | tf_op jit(solution)/shard_map/ppermute | solution.py:432
  98.9 0.7 collective-permute-done.38.refs_1_
  99.6 2.8 %shard_map.121 = (f32[512,128]{1,0:T(8,128)}, f32[256,128]{1,0:T(8,128)S(1)}, f32[256,128]{1,0:T(8,128)S(1)}) custom-call(s32[512]{0:T(512)S(1)} %pad_add_fusion.ids_ref, bf16[256,128,128]{2,1,0:T(8,128)(2,1)S(1)} %get-tuple-element.58.turned, f32[128,128]{1,0:T(8,128)S(1)} %add.73.refs_0_, f32[128,128]{1,0:T(8,128)S(1)} %collective-permute-done.38.refs_1_, ...), custom_call_target="tpu_custom_call" | custom-call | flops 8388608 | bytes 8388608 | tf_op jit(solution)/shard_map/pallas_call | solution.py:414
  102.4 1.3 %collective-permute-done.41 = f32[256,128]{1,0:T(8,128)S(1)} collective-permute-done((f32[256,128]{1,0:T(8,128)S(1)}, f32[256,128]{1,0:T(8,128)S(1)}, u32[]{:S(2)}, u32[]{:S(2)}) %collective-permute-start.41) | collective-permute-done | bytes 131104 | tf_op jit(solution)/shard_map/ppermute | solution.py:432
  103.8 1.3 %collective-permute-start.42 = (f32[256,128]{1,0:T(8,128)S(1)}, f32[256,128]{1,0:T(8,128)S(1)}, u32[]{:S(2)}, u32[]{:S(2)}) collective-permute-start(f32[256,128]{1,0:T(8,128)S(1)} %add.74), channel_id=1, source_target_pairs={{0,2},{1,3},{2,0},{3,1},{4,6},{5,7},{6,4},{7,5},{8,10},{9,11},{10,... | collective-permute-start | bytes 393224 | tf_op jit(solution)/shard_map/ppermute | solution.py:432
  105.1 4.3 %collective-permute-done.42 = f32[256,128]{1,0:T(8,128)S(1)} collective-permute-done((f32[256,128]{1,0:T(8,128)S(1)}, f32[256,128]{1,0:T(8,128)S(1)}, u32[]{:S(2)}, u32[]{:S(2)}) %collective-permute-start.42) | collective-permute-done | bytes 131104 | tf_op jit(solution)/shard_map/ppermute | solution.py:432
  109.5 1.3 %collective-permute-done.43.refs_1_ = f32[256,128]{1,0:T(8,128)S(1)} collective-permute-done((f32[256,128]{1,0:T(8,128)S(1)}, f32[256,128]{1,0:T(8,128)S(1)}, u32[]{:S(2)}, u32[]{:S(2)}) %collective-permute-start.43) | collective-permute-done | bytes 131104 | tf_op jit(solution)/shard_map/ppermute | solution.py:432
  110.9 0.9 shard_map.122
  (69 shorter events, 1.3 us)
Async XLA Ops:
  0.6 13.9 %copy-start.2 = (f32[65536]{0:T(1024)S(1)}, f32[65536]{0:T(1024)}, u32[]{:S(2)}) copy-start(f32[65536]{0:T(1024)} %param.19) | copy-start | bytes 786436
  7.0 4.2 %collective-permute-start = (f32[256,128]{1,0:T(8,128)S(1)}, f32[256,128]{1,0:T(8,128)S(1)}, u32[]{:S(2)}, u32[]{:S(2)}) collective-permute-start(f32[256,128]{1,0:T(8,128)S(1)} %get-tuple-element.56), channel_id=1, source_target_pairs={{0,1},{1,0},{2,3},{3,2},{4,5},{5,4},{6,7},{7,6},{8,9},{9,8},{10,11... | collective-permute-start | bytes 393224 | tf_op jit(solution)/shard_map/ppermute | solution.py:432
  7.6 10.0 %collective-permute-start.5 = (f32[128,128]{1,0:T(8,128)S(1)}, f32[128,128]{1,0:T(8,128)S(1)}, u32[]{:S(2)}, u32[]{:S(2)}) collective-permute-start(f32[128,128]{1,0:T(8,128)S(1)} %get-tuple-element.64), channel_id=1, source_target_pairs={{0,12},{4,8},{8,4},{12,0},{16,28},{20,24},{24,20},{28,16},{1,13},{... | collective-permute-start | bytes 196616 | tf_op jit(solution)/shard_map/ppermute | solution.py:432
  11.2 6.4 %collective-permute-start.3 = (f32[128,128]{1,0:T(8,128)S(1)}, f32[128,128]{1,0:T(8,128)S(1)}, u32[]{:S(2)}, u32[]{:S(2)}) collective-permute-start(f32[128,128]{1,0:T(8,128)S(1)} %get-tuple-element.62), channel_id=1, source_target_pairs={{0,4},{4,0},{8,12},{12,8},{16,20},{20,16},{24,28},{28,24},{1,5},{5... | collective-permute-start | bytes 196616 | tf_op jit(solution)/shard_map/ppermute | solution.py:432
  11.7 5.9 %collective-permute-start.4 = (f32[128,128]{1,0:T(8,128)S(1)}, f32[128,128]{1,0:T(8,128)S(1)}, u32[]{:S(2)}, u32[]{:S(2)}) collective-permute-start(f32[128,128]{1,0:T(8,128)S(1)} %get-tuple-element.63), channel_id=1, source_target_pairs={{0,8},{4,12},{8,0},{12,4},{16,24},{20,28},{24,16},{28,20},{1,9},{5... | collective-permute-start | bytes 196616 | tf_op jit(solution)/shard_map/ppermute | solution.py:432
  13.1 7.3 %collective-permute-start.1 = (f32[256,128]{1,0:T(8,128)S(1)}, f32[256,128]{1,0:T(8,128)S(1)}, u32[]{:S(2)}, u32[]{:S(2)}) collective-permute-start(f32[256,128]{1,0:T(8,128)S(1)} %max.36), channel_id=1, source_target_pairs={{0,2},{1,3},{2,0},{3,1},{4,6},{5,7},{6,4},{7,5},{8,10},{9,11},{10,... | collective-permute-start | bytes 393224 | tf_op jit(solution)/shard_map/ppermute | solution.py:432
  17.6 6.3 %collective-permute-start.6 = (f32[128,128]{1,0:T(8,128)S(1)}, f32[128,128]{1,0:T(8,128)S(1)}, u32[]{:S(2)}, u32[]{:S(2)}) collective-permute-start(f32[128,128]{1,0:T(8,128)S(1)} %maximum_maximum_fusion.1), channel_id=1, source_target_pairs={{0,16},{4,20},{8,24},{12,28},{16,0},{20,4},{24,8},{28,12},{1,17},{... | collective-permute-start | bytes 196616 | tf_op jit(solution)/shard_map/ppermute | solution.py:432
  20.4 5.3 %collective-permute-start.14 = (f32[128,128]{1,0:T(8,128)S(1)}, f32[128,128]{1,0:T(8,128)S(1)}, u32[]{:S(2)}, u32[]{:S(2)}) collective-permute-start(f32[128,128]{1,0:T(8,128)S(1)} %get-tuple-element.81), channel_id=1, source_target_pairs={{0,4},{4,0},{8,12},{12,8},{16,20},{20,16},{24,28},{28,24},{1,5},{5... | collective-permute-start | bytes 196616 | tf_op jit(solution)/shard_map/ppermute | solution.py:432
  21.1 5.0 %collective-permute-start.15 = (f32[128,128]{1,0:T(8,128)S(1)}, f32[128,128]{1,0:T(8,128)S(1)}, u32[]{:S(2)}, u32[]{:S(2)}) collective-permute-start(f32[128,128]{1,0:T(8,128)S(1)} %get-tuple-element.82), channel_id=1, source_target_pairs={{0,8},{4,12},{8,0},{12,4},{16,24},{20,28},{24,16},{28,20},{1,9},{5... | collective-permute-start | bytes 196616 | tf_op jit(solution)/shard_map/ppermute | solution.py:432
  22.7 5.2 %collective-permute-start.16 = (f32[128,128]{1,0:T(8,128)S(1)}, f32[128,128]{1,0:T(8,128)S(1)}, u32[]{:S(2)}, u32[]{:S(2)}) collective-permute-start(f32[128,128]{1,0:T(8,128)S(1)} %get-tuple-element.83), channel_id=1, source_target_pairs={{0,12},{4,8},{8,4},{12,0},{16,28},{20,24},{24,20},{28,16},{1,13},{... | collective-permute-start | bytes 196616 | tf_op jit(solution)/shard_map/ppermute | solution.py:432
  24.0 5.8 %collective-permute-start.2 = (f32[256,128]{1,0:T(8,128)S(1)}, f32[256,128]{1,0:T(8,128)S(1)}, u32[]{:S(2)}, u32[]{:S(2)}) collective-permute-start(f32[256,128]{1,0:T(8,128)S(1)} %max.37.refs_0_), channel_id=1, source_target_pairs={{0,1},{1,0},{2,3},{3,2},{4,5},{5,4},{6,7},{7,6},{8,9},{9,8},{10,11... | collective-permute-start | bytes 393224 | tf_op jit(solution)/shard_map/ppermute | solution.py:432
  24.0 9.9 %collective-permute-start.9 = (f32[128,128]{1,0:T(8,128)S(1)}, f32[128,128]{1,0:T(8,128)S(1)}, u32[]{:S(2)}, u32[]{:S(2)}) collective-permute-start(f32[128,128]{1,0:T(8,128)S(1)} %max.41.refs_0_), channel_id=1, source_target_pairs={{0,12},{4,8},{8,4},{12,0},{16,28},{20,24},{24,20},{28,16},{1,13},{... | collective-permute-start | bytes 196616 | tf_op jit(solution)/shard_map/ppermute | solution.py:432
  25.7 8.2 %collective-permute-start.8 = (f32[128,128]{1,0:T(8,128)S(1)}, f32[128,128]{1,0:T(8,128)S(1)}, u32[]{:S(2)}, u32[]{:S(2)}) collective-permute-start(f32[128,128]{1,0:T(8,128)S(1)} %max.41.refs_0_), channel_id=1, source_target_pairs={{0,8},{4,12},{8,0},{12,4},{16,24},{20,28},{24,16},{28,20},{1,9},{5... | collective-permute-start | bytes 196616 | tf_op jit(solution)/shard_map/ppermute | solution.py:432
  26.2 7.7 %collective-permute-start.7 = (f32[128,128]{1,0:T(8,128)S(1)}, f32[128,128]{1,0:T(8,128)S(1)}, u32[]{:S(2)}, u32[]{:S(2)}) collective-permute-start(f32[128,128]{1,0:T(8,128)S(1)} %max.41.refs_0_), channel_id=1, source_target_pairs={{0,4},{4,0},{8,12},{12,8},{16,20},{20,16},{24,28},{28,24},{1,5},{5... | collective-permute-start | bytes 196616 | tf_op jit(solution)/shard_map/ppermute | solution.py:432
  27.9 13.7 %collective-permute-start.17 = (f32[128,128]{1,0:T(8,128)S(1)}, f32[128,128]{1,0:T(8,128)S(1)}, u32[]{:S(2)}, u32[]{:S(2)}) collective-permute-start(f32[128,128]{1,0:T(8,128)S(1)} %add_add_fusion.1), channel_id=1, source_target_pairs={{0,16},{4,20},{8,24},{12,28},{16,0},{20,4},{24,8},{28,12},{1,17},{... | collective-permute-start | bytes 196616 | tf_op jit(solution)/shard_map/ppermute | solution.py:432
  33.9 19.6 %copy-start = (f32[65536]{0:T(1024)S(1)}, f32[65536]{0:T(1024)}, u32[]{:S(2)}) copy-start(f32[65536]{0:T(1024)} %param.14) | copy-start | bytes 786436
  33.9 27.8 %copy-start.1 = (f32[65536]{0:T(1024)S(1)}, f32[65536]{0:T(1024)}, u32[]{:S(2)}) copy-start(f32[65536]{0:T(1024)} %param.13) | copy-start | bytes 786436
  33.9 31.7 %copy-start.3 = (f32[65536]{0:T(1024)S(1)}, f32[65536]{0:T(1024)}, u32[]{:S(2)}) copy-start(f32[65536]{0:T(1024)} %param.15) | copy-start | bytes 786436
  33.9 31.7 %copy-start.4 = (f32[65536]{0:T(1024)S(1)}, f32[65536]{0:T(1024)}, u32[]{:S(2)}) copy-start(f32[65536]{0:T(1024)} %param.16) | copy-start | bytes 786436
  33.9 31.7 %copy-start.5 = (s32[65536]{0:T(1024)S(1)}, s32[65536]{0:T(1024)}, u32[]{:S(2)}) copy-start(s32[65536]{0:T(1024)} %param.17) | copy-start | bytes 786436
  34.0 31.7 %copy-start.6 = (f32[65536]{0:T(1024)S(1)}, f32[65536]{0:T(1024)}, u32[]{:S(2)}) copy-start(f32[65536]{0:T(1024)} %param.18) | copy-start | bytes 786436
  34.0 7.7 %collective-permute-start.10 = (f32[128,128]{1,0:T(8,128)S(1)}, f32[128,128]{1,0:T(8,128)S(1)}, u32[]{:S(2)}, u32[]{:S(2)}) collective-permute-start(f32[128,128]{1,0:T(8,128)S(1)} %get-tuple-element.77), channel_id=1, source_target_pairs={{0,4},{4,0},{8,12},{12,8},{16,20},{20,16},{24,28},{28,24},{1,5},{5... | collective-permute-start | bytes 196616 | tf_op jit(solution)/shard_map/ppermute | solution.py:432
  34.8 6.9 %collective-permute-start.11 = (f32[128,128]{1,0:T(8,128)S(1)}, f32[128,128]{1,0:T(8,128)S(1)}, u32[]{:S(2)}, u32[]{:S(2)}) collective-permute-start(f32[128,128]{1,0:T(8,128)S(1)} %get-tuple-element.78), channel_id=1, source_target_pairs={{0,8},{4,12},{8,0},{12,4},{16,24},{20,28},{24,16},{28,20},{1,9},{5... | collective-permute-start | bytes 196616 | tf_op jit(solution)/shard_map/ppermute | solution.py:432
  36.4 5.3 %collective-permute-start.12 = (f32[128,128]{1,0:T(8,128)S(1)}, f32[128,128]{1,0:T(8,128)S(1)}, u32[]{:S(2)}, u32[]{:S(2)}) collective-permute-start(f32[128,128]{1,0:T(8,128)S(1)} %get-tuple-element.79), channel_id=1, source_target_pairs={{0,12},{4,8},{8,4},{12,0},{16,28},{20,24},{24,20},{28,16},{1,13},{... | collective-permute-start | bytes 196616 | tf_op jit(solution)/shard_map/ppermute | solution.py:432
  41.7 1.4 %collective-permute-start.21 = (f32[256,128]{1,0:T(8,128)S(1)}, f32[256,128]{1,0:T(8,128)S(1)}, u32[]{:S(2)}, u32[]{:S(2)}) collective-permute-start(f32[256,128]{1,0:T(8,128)S(1)} %get-tuple-element.90), channel_id=1, source_target_pairs={{0,1},{1,0},{2,3},{3,2},{4,5},{5,4},{6,7},{7,6},{8,9},{9,8},{10,11... | collective-permute-start | bytes 393224 | tf_op jit(solution)/shard_map/ppermute | solution.py:432
  43.1 6.6 %collective-permute-start.22 = (f32[256,128]{1,0:T(8,128)S(1)}, f32[256,128]{1,0:T(8,128)S(1)}, u32[]{:S(2)}, u32[]{:S(2)}) collective-permute-start(f32[256,128]{1,0:T(8,128)S(1)} %max.46), channel_id=1, source_target_pairs={{0,2},{1,3},{2,0},{3,1},{4,6},{5,7},{6,4},{7,5},{8,10},{9,11},{10,... | collective-permute-start | bytes 393224 | tf_op jit(solution)/shard_map/ppermute | solution.py:432
  43.8 6.0 %collective-permute-start.13 = (f32[128,128]{1,0:T(8,128)S(1)}, f32[128,128]{1,0:T(8,128)S(1)}, u32[]{:S(2)}, u32[]{:S(2)}) collective-permute-start(f32[128,128]{1,0:T(8,128)S(1)} %maximum_maximum_fusion), channel_id=1, source_target_pairs={{0,16},{4,20},{8,24},{12,28},{16,0},{20,4},{24,8},{28,12},{1,17},{... | collective-permute-start | bytes 196616 | tf_op jit(solution)/shard_map/ppermute | solution.py:432
  49.8 3.7 %collective-permute-start.23 = (f32[256,128]{1,0:T(8,128)S(1)}, f32[256,128]{1,0:T(8,128)S(1)}, u32[]{:S(2)}, u32[]{:S(2)}) collective-permute-start(f32[256,128]{1,0:T(8,128)S(1)} %max.47.near), channel_id=1, source_target_pairs={{0,1},{1,0},{2,3},{3,2},{4,5},{5,4},{6,7},{7,6},{8,9},{9,8},{10,11... | collective-permute-start | bytes 393224 | tf_op jit(solution)/shard_map/ppermute | solution.py:432
  49.9 10.6 %collective-permute-start.20 = (f32[256,128]{1,0:T(8,128)S(1)}, f32[256,128]{1,0:T(8,128)S(1)}, u32[]{:S(2)}, u32[]{:S(2)}) collective-permute-start(f32[256,128]{1,0:T(8,128)S(1)} %pad_maximum_fusion.refs_0_), channel_id=1, source_target_pairs={{0,12},{4,8},{8,4},{12,0},{16,28},{20,24},{24,20},{28,16},{1,13},{... | collective-permute-start | bytes 393224 | tf_op jit(solution)/shard_map/ppermute | solution.py:432
  50.9 10.8 %collective-permute-start.19 = (f32[256,128]{1,0:T(8,128)S(1)}, f32[256,128]{1,0:T(8,128)S(1)}, u32[]{:S(2)}, u32[]{:S(2)}) collective-permute-start(f32[256,128]{1,0:T(8,128)S(1)} %pad_maximum_fusion.refs_0_), channel_id=1, source_target_pairs={{0,8},{4,12},{8,0},{12,4},{16,24},{20,28},{24,16},{28,20},{1,9},{5... | collective-permute-start | bytes 393224 | tf_op jit(solution)/shard_map/ppermute | solution.py:432
  52.7 9.0 %collective-permute-start.18 = (f32[256,128]{1,0:T(8,128)S(1)}, f32[256,128]{1,0:T(8,128)S(1)}, u32[]{:S(2)}, u32[]{:S(2)}) collective-permute-start(f32[256,128]{1,0:T(8,128)S(1)} %pad_maximum_fusion.refs_0_), channel_id=1, source_target_pairs={{0,4},{4,0},{8,12},{12,8},{16,20},{20,16},{24,28},{28,24},{1,5},{5... | collective-permute-start | bytes 393224 | tf_op jit(solution)/shard_map/ppermute | solution.py:432
  53.5 4.7 %collective-permute-start.24 = (f32[8,128]{1,0:T(8,128)S(1)}, f32[8,128]{1,0:T(8,128)S(1)}, u32[]{:S(2)}, u32[]{:S(2)}) collective-permute-start(f32[8,128]{1,0:T(8,128)S(1)} %get-tuple-element.92), channel_id=1, source_target_pairs={{0,16},{4,20},{8,24},{12,28},{16,0},{20,4},{24,8},{28,12},{1,17},{... | collective-permute-start | bytes 12296 | tf_op jit(solution)/shard_map/ppermute | solution.py:432
  58.2 3.6 %collective-permute-start.25 = (f32[8,128]{1,0:T(8,128)S(1)}, f32[8,128]{1,0:T(8,128)S(1)}, u32[]{:S(2)}, u32[]{:S(2)}) collective-permute-start(f32[8,128]{1,0:T(8,128)S(1)} %add.61), channel_id=1, source_target_pairs={{0,4},{4,0},{8,12},{12,8},{16,20},{20,16},{24,28},{28,24},{1,5},{5... | collective-permute-start | bytes 12296 | tf_op jit(solution)/shard_map/ppermute | solution.py:432
  59.5 4.5 %collective-permute-start.30 = (f32[8,128]{1,0:T(8,128)S(1)}, f32[8,128]{1,0:T(8,128)S(1)}, u32[]{:S(2)}, u32[]{:S(2)}) collective-permute-start(f32[8,128]{1,0:T(8,128)S(1)} %add.61), channel_id=1, source_target_pairs={{0,12},{4,8},{8,4},{12,0},{16,28},{20,24},{24,20},{28,16},{1,13},{... | collective-permute-start | bytes 12296 | tf_op jit(solution)/shard_map/ppermute | solution.py:432
  60.5 3.6 %collective-permute-start.29 = (f32[8,128]{1,0:T(8,128)S(1)}, f32[8,128]{1,0:T(8,128)S(1)}, u32[]{:S(2)}, u32[]{:S(2)}) collective-permute-start(f32[8,128]{1,0:T(8,128)S(1)} %add.61), channel_id=1, source_target_pairs={{0,8},{4,12},{8,0},{12,4},{16,24},{20,28},{24,16},{28,20},{1,9},{5... | collective-permute-start | bytes 12296 | tf_op jit(solution)/shard_map/ppermute | solution.py:432
  61.8 3.1 %collective-permute-start.28 = (f32[8,128]{1,0:T(8,128)S(1)}, f32[8,128]{1,0:T(8,128)S(1)}, u32[]{:S(2)}, u32[]{:S(2)}) collective-permute-start(f32[8,128]{1,0:T(8,128)S(1)} %get-tuple-element.93), channel_id=1, source_target_pairs={{0,3},{1,2},{2,1},{3,0},{4,7},{5,6},{6,5},{7,4},{8,11},{9,10},{10,... | collective-permute-start | bytes 12296 | tf_op jit(solution)/shard_map/ppermute | solution.py:432
  61.9 3.7 %collective-permute-start.27 = (f32[8,128]{1,0:T(8,128)S(1)}, f32[8,128]{1,0:T(8,128)S(1)}, u32[]{:S(2)}, u32[]{:S(2)}) collective-permute-start(f32[8,128]{1,0:T(8,128)S(1)} %get-tuple-element.93), channel_id=1, source_target_pairs={{0,2},{1,3},{2,0},{3,1},{4,6},{5,7},{6,4},{7,5},{8,10},{9,11},{10,... | collective-permute-start | bytes 12296 | tf_op jit(solution)/shard_map/ppermute | solution.py:432
  63.5 2.1 %collective-permute-start.26 = (f32[8,128]{1,0:T(8,128)S(1)}, f32[8,128]{1,0:T(8,128)S(1)}, u32[]{:S(2)}, u32[]{:S(2)}) collective-permute-start(f32[8,128]{1,0:T(8,128)S(1)} %get-tuple-element.93), channel_id=1, source_target_pairs={{0,1},{1,0},{2,3},{3,2},{4,5},{5,4},{6,7},{7,6},{8,9},{9,8},{10,11... | collective-permute-start | bytes 12296 | tf_op jit(solution)/shard_map/ppermute | solution.py:432
  68.4 1.6 %collective-permute-start.31 = (f32[256,128]{1,0:T(8,128)S(1)}, f32[256,128]{1,0:T(8,128)S(1)}, u32[]{:S(2)}, u32[]{:S(2)}) collective-permute-start(f32[256,128]{1,0:T(8,128)S(1)} %get-tuple-element.95), channel_id=1, source_target_pairs={{0,1},{1,0},{2,3},{3,2},{4,5},{5,4},{6,7},{7,6},{8,9},{9,8},{10,11... | collective-permute-start | bytes 393224 | tf_op jit(solution)/shard_map/ppermute | solution.py:432
  70.0 5.8 %collective-permute-start.32 = (f32[256,128]{1,0:T(8,128)S(1)}, f32[256,128]{1,0:T(8,128)S(1)}, u32[]{:S(2)}, u32[]{:S(2)}) collective-permute-start(f32[256,128]{1,0:T(8,128)S(1)} %add.68), channel_id=1, source_target_pairs={{0,2},{1,3},{2,0},{3,1},{4,6},{5,7},{6,4},{7,5},{8,10},{9,11},{10,... | collective-permute-start | bytes 393224 | tf_op jit(solution)/shard_map/ppermute | solution.py:432
  75.9 1.4 %collective-permute-start.33 = (f32[256,128]{1,0:T(8,128)S(1)}, f32[256,128]{1,0:T(8,128)S(1)}, u32[]{:S(2)}, u32[]{:S(2)}) collective-permute-start(f32[256,128]{1,0:T(8,128)S(1)} %add.69.refs_0_), channel_id=1, source_target_pairs={{0,1},{1,0},{2,3},{3,2},{4,5},{5,4},{6,7},{7,6},{8,9},{9,8},{10,11... | collective-permute-start | bytes 393224 | tf_op jit(solution)/shard_map/ppermute | solution.py:432
  79.9 4.4 %collective-permute-start.34 = (f32[128,128]{1,0:T(8,128)S(1)}, f32[128,128]{1,0:T(8,128)S(1)}, u32[]{:S(2)}, u32[]{:S(2)}) collective-permute-start(f32[128,128]{1,0:T(8,128)S(1)} %get-tuple-element.98), channel_id=1, source_target_pairs={{0,4},{4,0},{8,12},{12,8},{16,20},{20,16},{24,28},{28,24},{1,5},{5... | collective-permute-start | bytes 196616 | tf_op jit(solution)/shard_map/ppermute | solution.py:432
  81.2 4.6 %collective-permute-start.35 = (f32[128,128]{1,0:T(8,128)S(1)}, f32[128,128]{1,0:T(8,128)S(1)}, u32[]{:S(2)}, u32[]{:S(2)}) collective-permute-start(f32[128,128]{1,0:T(8,128)S(1)} %get-tuple-element.99), channel_id=1, source_target_pairs={{0,8},{4,12},{8,0},{12,4},{16,24},{20,28},{24,16},{28,20},{1,9},{5... | collective-permute-start | bytes 196616 | tf_op jit(solution)/shard_map/ppermute | solution.py:432
  82.4 5.2 %collective-permute-start.36 = (f32[128,128]{1,0:T(8,128)S(1)}, f32[128,128]{1,0:T(8,128)S(1)}, u32[]{:S(2)}, u32[]{:S(2)}) collective-permute-start(f32[128,128]{1,0:T(8,128)S(1)} %get-tuple-element.100), channel_id=1, source_target_pairs={{0,12},{4,8},{8,4},{12,0},{16,28},{20,24},{24,20},{28,16},{1,13},{... | collective-permute-start | bytes 196616 | tf_op jit(solution)/shard_map/ppermute | solution.py:432
  87.6 6.0 %collective-permute-start.37 = (f32[128,128]{1,0:T(8,128)S(1)}, f32[128,128]{1,0:T(8,128)S(1)}, u32[]{:S(2)}, u32[]{:S(2)}) collective-permute-start(f32[128,128]{1,0:T(8,128)S(1)} %add_add_fusion), channel_id=1, source_target_pairs={{0,16},{4,20},{8,24},{12,28},{16,0},{20,4},{24,8},{28,12},{1,17},{... | collective-permute-start | bytes 196616 | tf_op jit(solution)/shard_map/ppermute | solution.py:432
  93.7 5.2 %collective-permute-start.40 = (f32[128,128]{1,0:T(8,128)S(1)}, f32[128,128]{1,0:T(8,128)S(1)}, u32[]{:S(2)}, u32[]{:S(2)}) collective-permute-start(f32[128,128]{1,0:T(8,128)S(1)} %add.73.refs_0_), channel_id=1, source_target_pairs={{0,12},{4,8},{8,4},{12,0},{16,28},{20,24},{24,20},{28,16},{1,13},{... | collective-permute-start | bytes 196616 | tf_op jit(solution)/shard_map/ppermute | solution.py:432
  94.2 4.8 %collective-permute-start.39 = (f32[128,128]{1,0:T(8,128)S(1)}, f32[128,128]{1,0:T(8,128)S(1)}, u32[]{:S(2)}, u32[]{:S(2)}) collective-permute-start(f32[128,128]{1,0:T(8,128)S(1)} %add.73.refs_0_), channel_id=1, source_target_pairs={{0,8},{4,12},{8,0},{12,4},{16,24},{20,28},{24,16},{28,20},{1,9},{5... | collective-permute-start | bytes 196616 | tf_op jit(solution)/shard_map/ppermute | solution.py:432
  94.7 4.8 %collective-permute-start.38 = (f32[128,128]{1,0:T(8,128)S(1)}, f32[128,128]{1,0:T(8,128)S(1)}, u32[]{:S(2)}, u32[]{:S(2)}) collective-permute-start(f32[128,128]{1,0:T(8,128)S(1)} %add.73.refs_0_), channel_id=1, source_target_pairs={{0,4},{4,0},{8,12},{12,8},{16,20},{20,16},{24,28},{28,24},{1,5},{5... | collective-permute-start | bytes 196616 | tf_op jit(solution)/shard_map/ppermute | solution.py:432
  102.4 1.4 %collective-permute-start.41 = (f32[256,128]{1,0:T(8,128)S(1)}, f32[256,128]{1,0:T(8,128)S(1)}, u32[]{:S(2)}, u32[]{:S(2)}) collective-permute-start(f32[256,128]{1,0:T(8,128)S(1)} %get-tuple-element.104), channel_id=1, source_target_pairs={{0,1},{1,0},{2,3},{3,2},{4,5},{5,4},{6,7},{7,6},{8,9},{9,8},{10,11... | collective-permute-start | bytes 393224 | tf_op jit(solution)/shard_map/ppermute | solution.py:432
  103.8 5.6 %collective-permute-start.42 = (f32[256,128]{1,0:T(8,128)S(1)}, f32[256,128]{1,0:T(8,128)S(1)}, u32[]{:S(2)}, u32[]{:S(2)}) collective-permute-start(f32[256,128]{1,0:T(8,128)S(1)} %add.74), channel_id=1, source_target_pairs={{0,2},{1,3},{2,0},{3,1},{4,6},{5,7},{6,4},{7,5},{8,10},{9,11},{10,... | collective-permute-start | bytes 393224 | tf_op jit(solution)/shard_map/ppermute | solution.py:432
  109.4 1.4 %collective-permute-start.43 = (f32[256,128]{1,0:T(8,128)S(1)}, f32[256,128]{1,0:T(8,128)S(1)}, u32[]{:S(2)}, u32[]{:S(2)}) collective-permute-start(f32[256,128]{1,0:T(8,128)S(1)} %add.75.refs_0_), channel_id=1, source_target_pairs={{0,1},{1,0},{2,3},{3,2},{4,5},{5,4},{6,7},{7,6},{8,9},{9,8},{10,11... | collective-permute-start | bytes 393224 | tf_op jit(solution)/shard_map/ppermute | solution.py:432
where the time goes:
time: 112 us
  starting transfers between devices  46.4 us (41%)
  waiting for transfers between devices  37.3 us (33%)
  Pallas kernels  26 us (23%)
    ppermute x44, starting transfers between devices, swap(): return lax.ppermute(vector, axis, [(i, i ^ bit) for i in range(size)])  46.4 us
    ppermute x44, waiting for transfers between devices, swap(): return lax.ppermute(vector, axis, [(i, i ^ bit) for i in range(size)])  37.3 us
    pallas_call x7, Pallas kernels, call_blocks(): pl.pallas_call(kernel, out_shape=out_shape, in_specs=[pl.BlockSpec(memory...  25 us
  transfers between devices with their start and end apart: 44, of which 20 were waited for; matrix products, arithmetic and copies ran while one was open for 0% of the time, Pallas kernels for 10%

commit v1 on v0

--- a/solution.py
+++ b/solution.py
@@ -12,7 +12,7 @@
 
 CHUNKS = 8
 FIRST_GROUP = 32
-GROUP = 64
+GROUP = 128
 AHEAD = 3
 ROW_HALVING = 1
 QUARTERS = 4
@@ -555,7 +555,7 @@
     )
     col_peaks = gather_cols(share, row_groups)
     share = scatter_cols(after(col_pieces_2, col_peaks), row_groups, jnp.maximum)
-    product = exchange_cols(product, row_groups, jnp.add)
+    product = exchange_cols(after(product, col_pieces_2), row_groups, jnp.add)
     near, far, col_scale = call_blocks(
         functools.partial(second_rows_kernel, count),
         ids,

time: 112 us -> 111 us (level)
  transfers between devices with their start and end apart: 44 -> 44, of which waited for: 20 -> 19; matrix products, arithmetic and copies ran while one was open for 0% -> 0% of each run, Pallas kernels for 10% -> 10%
where the time goes in v1:
time: 111 us
  starting transfers between devices  46.3 us (42%)
  waiting for transfers between devices  36.7 us (33%)
  Pallas kernels  25.8 us (23%)
    ppermute x44, starting transfers between devices, swap(): return lax.ppermute(vector, axis, [(i, i ^ bit) for i in range(size)])  46.3 us
    ppermute x44, waiting for transfers between devices, swap(): return lax.ppermute(vector, axis, [(i, i ^ bit) for i in range(size)])  36.7 us
    pallas_call x7, Pallas kernels, call_blocks(): pl.pallas_call(kernel, out_shape=out_shape, in_specs=[pl.BlockSpec(memory...  24.7 us
  transfers between devices with their start and end apart: 44, of which 19 were waited for; matrix products, arithmetic and copies ran while one was open for 0% of the time, Pallas kernels for 10%

profile of v1, /device:TPU:0, one launch (start us, length us, event | category | flops | bytes accessed | tf_op | source)
XLA Modules:
  0.0 110.8 jit_solution(11961144265114079394)
XLA Ops:
  0.6 0.7 pad_add_fusion.ids_ref
  1.4 5.7 %shard_map.113 = (f32[256,128]{1,0:T(8,128)S(1)}, f32[256,128]{1,0:T(8,128)S(1)}, f32[128,128]{1,0:T(8,128)S(1)}, f32[128,128]{1,0:T(8,128)S(1)}, f32[128,128]{1...) custom-call(s32[512]{0:T(512)S(1)} %pad_add_fusion.ids_ref, bf16[256,128,128]{2,1,0:T(8,128)(2,1)} %bitcast.27), custom_call_target="tpu_custom_call" | custom-call | flops 8388608 | bytes 8388608 | tf_op jit(solution)/shard_map/pallas_call | solution.py:414
  7.1 0.5 collective-permute-start
  7.6 3.5 %collective-permute-start.5 = (f32[128,128]{1,0:T(8,128)S(1)}, f32[128,128]{1,0:T(8,128)S(1)}, u32[]{:S(2)}, u32[]{:S(2)}) collective-permute-start(f32[128,128]{1,0:T(8,128)S(1)} %get-tuple-element.65), channel_id=1, source_target_pairs={{0,12},{4,8},{8,4},{12,0},{16,28},{20,24},{24,20},{28,16},{1,13},{... | collective-permute-start | bytes 196616 | tf_op jit(solution)/shard_map/ppermute | solution.py:432
  11.1 0.6 collective-permute-start.3
  11.7 1.2 %collective-permute-start.4 = (f32[128,128]{1,0:T(8,128)S(1)}, f32[128,128]{1,0:T(8,128)S(1)}, u32[]{:S(2)}, u32[]{:S(2)}) collective-permute-start(f32[128,128]{1,0:T(8,128)S(1)} %get-tuple-element.64), channel_id=1, source_target_pairs={{0,8},{4,12},{8,0},{12,4},{16,24},{20,28},{24,16},{28,20},{1,9},{5... | collective-permute-start | bytes 196616 | tf_op jit(solution)/shard_map/ppermute | solution.py:432
  13.0 1.5 %collective-permute-start.1 = (f32[256,128]{1,0:T(8,128)S(1)}, f32[256,128]{1,0:T(8,128)S(1)}, u32[]{:S(2)}, u32[]{:S(2)}) collective-permute-start(f32[256,128]{1,0:T(8,128)S(1)} %max.36), channel_id=1, source_target_pairs={{0,2},{1,3},{2,0},{3,1},{4,6},{5,7},{6,4},{7,5},{8,10},{9,11},{10,... | collective-permute-start | bytes 393224 | tf_op jit(solution)/shard_map/ppermute | solution.py:432
  14.5 3.1 %shard_map.114 = (f32[128,128]{1,0:T(8,128)S(1)}, f32[128,128]{1,0:T(8,128)S(1)}, f32[128,128]{1,0:T(8,128)S(1)}, f32[128,128]{1,0:T(8,128)S(1)}, bf16[256,128,128]{2,1,0:T(8,128)(2,1)S(1)}) custom-call(s32[512]{0:T(512)S(1)} %pad_add_fusion.ids_ref, bf16[256,128,128]{2,1,0:T(8,128)(2,1)S(1)} %get-tuple-element.55.blocks, f32[512,128]{1,0:T(8,128)S(1)} %bitcast.18), custom_call_target="tpu_custom_call" | custom-call | flops 8388608 | bytes 8388608 | tf_op jit(solution)/shard_map/pallas_call | solution.py:414
  17.7 2.7 %collective-permute-start.6 = (f32[128,128]{1,0:T(8,128)S(1)}, f32[128,128]{1,0:T(8,128)S(1)}, u32[]{:S(2)}, u32[]{:S(2)}) collective-permute-start(f32[128,128]{1,0:T(8,128)S(1)} %maximum_maximum_fusion.1), channel_id=1, source_target_pairs={{0,16},{4,20},{8,24},{12,28},{16,0},{20,4},{24,8},{28,12},{1,17},{... | collective-permute-start | bytes 196616 | tf_op jit(solution)/shard_map/ppermute | solution.py:432
  20.4 0.7 collective-permute-start.14
  21.1 1.6 %collective-permute-start.15 = (f32[128,128]{1,0:T(8,128)S(1)}, f32[128,128]{1,0:T(8,128)S(1)}, u32[]{:S(2)}, u32[]{:S(2)}) collective-permute-start(f32[128,128]{1,0:T(8,128)S(1)} %get-tuple-element.83), channel_id=1, source_target_pairs={{0,8},{4,12},{8,0},{12,4},{16,24},{20,28},{24,16},{28,20},{1,9},{5... | collective-permute-start | bytes 196616 | tf_op jit(solution)/shard_map/ppermute | solution.py:432
  22.7 1.2 %collective-permute-start.16 = (f32[128,128]{1,0:T(8,128)S(1)}, f32[128,128]{1,0:T(8,128)S(1)}, u32[]{:S(2)}, u32[]{:S(2)}) collective-permute-start(f32[128,128]{1,0:T(8,128)S(1)} %get-tuple-element.84), channel_id=1, source_target_pairs={{0,12},{4,8},{8,4},{12,0},{16,28},{20,24},{24,20},{28,16},{1,13},{... | collective-permute-start | bytes 196616 | tf_op jit(solution)/shard_map/ppermute | solution.py:432
  24.0 1.8 %collective-permute-start.9 = (f32[128,128]{1,0:T(8,128)S(1)}, f32[128,128]{1,0:T(8,128)S(1)}, u32[]{:S(2)}, u32[]{:S(2)}) collective-permute-start(f32[128,128]{1,0:T(8,128)S(1)} %max.41.refs_0_), channel_id=1, source_target_pairs={{0,12},{4,8},{8,4},{12,0},{16,28},{20,24},{24,20},{28,16},{1,13},{... | collective-permute-start | bytes 196616 | tf_op jit(solution)/shard_map/ppermute | solution.py:432
  25.7 0.4 collective-permute-start.8
  26.2 1.5 %collective-permute-start.7 = (f32[128,128]{1,0:T(8,128)S(1)}, f32[128,128]{1,0:T(8,128)S(1)}, u32[]{:S(2)}, u32[]{:S(2)}) collective-permute-start(f32[128,128]{1,0:T(8,128)S(1)} %max.41.refs_0_), channel_id=1, source_target_pairs={{0,4},{4,0},{8,12},{12,8},{16,20},{20,16},{24,28},{28,24},{1,5},{5... | collective-permute-start | bytes 196616 | tf_op jit(solution)/shard_map/ppermute | solution.py:432
  27.7 0.2 collective-permute-done.16
  27.9 4.0 %shard_map.115 = (f32[128,128]{1,0:T(8,128)S(1)}, f32[128,128]{1,0:T(8,128)S(1)}, f32[128,128]{1,0:T(8,128)S(1)}, f32[128,128]{1,0:T(8,128)S(1)}, f32[512,128]{1,0:T(8,128)S(1)}) custom-call(s32[512]{0:T(512)S(1)} %pad_add_fusion.ids_ref, bf16[256,128,128]{2,1,0:T(8,128)(2,1)S(1)} %get-tuple-element.55.blocks, ...), custom_call_target="tpu_custom_call" | custom-call | flops 8388608 | bytes 8388608 | tf_op jit(solution)/shard_map/pallas_call | solution.py:414
  32.1 0.4 collective-permute-start.10
  32.4 2.2 %collective-permute-start.17 = (f32[128,128]{1,0:T(8,128)S(1)}, f32[128,128]{1,0:T(8,128)S(1)}, u32[]{:S(2)}, u32[]{:S(2)}) collective-permute-start(f32[128,128]{1,0:T(8,128)S(1)} %add_add_fusion.1), channel_id=1, source_target_pairs={{0,16},{4,20},{8,24},{12,28},{16,0},{20,4},{24,8},{28,12},{1,17},{... | collective-permute-start | bytes 196616 | tf_op jit(solution)/shard_map/ppermute | solution.py:432
  34.6 1.6 %collective-permute-start.11 = (f32[128,128]{1,0:T(8,128)S(1)}, f32[128,128]{1,0:T(8,128)S(1)}, u32[]{:S(2)}, u32[]{:S(2)}) collective-permute-start(f32[128,128]{1,0:T(8,128)S(1)} %get-tuple-element.79), channel_id=1, source_target_pairs={{0,8},{4,12},{8,0},{12,4},{16,24},{20,28},{24,16},{28,20},{1,9},{5... | collective-permute-start | bytes 196616 | tf_op jit(solution)/shard_map/ppermute | solution.py:432
  36.3 1.2 %collective-permute-start.12 = (f32[128,128]{1,0:T(8,128)S(1)}, f32[128,128]{1,0:T(8,128)S(1)}, u32[]{:S(2)}, u32[]{:S(2)}) collective-permute-start(f32[128,128]{1,0:T(8,128)S(1)} %get-tuple-element.80), channel_id=1, source_target_pairs={{0,12},{4,8},{8,4},{12,0},{16,28},{20,24},{24,20},{28,16},{1,13},{... | collective-permute-start | bytes 196616 | tf_op jit(solution)/shard_map/ppermute | solution.py:432
  37.5 4.0 %shard_map.116 = (f32[256,128]{1,0:T(8,128)S(1)}, f32[256,128]{1,0:T(8,128)S(1)}, f32[512,128]{1,0:T(8,128)S(1)}) custom-call(s32[512]{0:T(512)S(1)} %pad_add_fusion.ids_ref, bf16[256,128,128]{2,1,0:T(8,128)(2,1)S(1)} %get-tuple-element.55.blocks, bf16[256,128,128]{2,1,0:T(8,128)(2,1)S(1)} %get-tuple-element.59.turned, f32[128,128]{1,0:T(8,128)S(1)} %max.41.refs_0_, ...), custom_call_target="tpu_custom_call" | custom-call | flops 8388608 | bytes 8388608 | tf_op jit(solution)/shard_map/pallas_call | solution.py:414
  41.7 1.3 %collective-permute-done.21 = f32[256,128]{1,0:T(8,128)S(1)} collective-permute-done((f32[256,128]{1,0:T(8,128)S(1)}, f32[256,128]{1,0:T(8,128)S(1)}, u32[]{:S(2)}, u32[]{:S(2)}) %collective-permute-start.21) | collective-permute-done | bytes 131104 | tf_op jit(solution)/shard_map/ppermute | solution.py:432
  43.1 0.3 collective-permute-start.22
  43.4 1.2 %collective-permute-start.13 = (f32[128,128]{1,0:T(8,128)S(1)}, f32[128,128]{1,0:T(8,128)S(1)}, u32[]{:S(2)}, u32[]{:S(2)}) collective-permute-start(f32[128,128]{1,0:T(8,128)S(1)} %maximum_maximum_fusion), channel_id=1, source_target_pairs={{0,16},{4,20},{8,24},{12,28},{16,0},{20,4},{24,8},{28,12},{1,17},{... | collective-permute-start | bytes 196616 | tf_op jit(solution)/shard_map/ppermute | solution.py:432
  44.6 5.1 %collective-permute-done.13 = f32[128,128]{1,0:T(8,128)S(1)} collective-permute-done((f32[128,128]{1,0:T(8,128)S(1)}, f32[128,128]{1,0:T(8,128)S(1)}, u32[]{:S(2)}, u32[]{:S(2)}) %collective-permute-start.13) | collective-permute-done | bytes 65568 | tf_op jit(solution)/shard_map/ppermute | solution.py:432
  49.8 0.8 collective-permute-start.20
  50.6 1.8 %collective-permute-start.19 = (f32[256,128]{1,0:T(8,128)S(1)}, f32[256,128]{1,0:T(8,128)S(1)}, u32[]{:S(2)}, u32[]{:S(2)}) collective-permute-start(f32[256,128]{1,0:T(8,128)S(1)} %pad_maximum_fusion.refs_0_), channel_id=1, source_target_pairs={{0,8},{4,12},{8,0},{12,4},{16,24},{20,28},{24,16},{28,20},{1,9},{5... | collective-permute-start | bytes 393224 | tf_op jit(solution)/shard_map/ppermute | solution.py:432
  52.4 1.0 collective-permute-start.18
  53.6 4.5 %collective-permute-done.24 = f32[8,128]{1,0:T(8,128)S(1)} collective-permute-done((f32[8,128]{1,0:T(8,128)S(1)}, f32[8,128]{1,0:T(8,128)S(1)}, u32[]{:S(2)}, u32[]{:S(2)}) %collective-permute-start.24) | collective-permute-done | bytes 4128 | tf_op jit(solution)/shard_map/ppermute | solution.py:432
  58.1 1.0 collective-permute-start.25
  59.2 1.1 collective-permute-start.30
  60.3 1.4 %collective-permute-start.29 = (f32[8,128]{1,0:T(8,128)S(1)}, f32[8,128]{1,0:T(8,128)S(1)}, u32[]{:S(2)}, u32[]{:S(2)}) collective-permute-start(f32[8,128]{1,0:T(8,128)S(1)} %add.61), channel_id=1, source_target_pairs={{0,8},{4,12},{8,0},{12,4},{16,24},{20,28},{24,16},{28,20},{1,9},{5... | collective-permute-start | bytes 12296 | tf_op jit(solution)/shard_map/ppermute | solution.py:432
  61.8 1.4 %collective-permute-start.27 = (f32[8,128]{1,0:T(8,128)S(1)}, f32[8,128]{1,0:T(8,128)S(1)}, u32[]{:S(2)}, u32[]{:S(2)}) collective-permute-start(f32[8,128]{1,0:T(8,128)S(1)} %get-tuple-element.95), channel_id=1, source_target_pairs={{0,2},{1,3},{2,0},{3,1},{4,6},{5,7},{6,4},{7,5},{8,10},{9,11},{10,... | collective-permute-start | bytes 12296 | tf_op jit(solution)/shard_map/ppermute | solution.py:432
  63.2 0.4 collective-permute-start.26
  63.7 0.2 collective-permute-done.29
  63.9 0.9 collective-permute-done.28
  64.8 0.7 collective-permute-done.27
  65.5 2.7 %shard_map.119 = (f32[512,128]{1,0:T(8,128)S(1)}, f32[256,128]{1,0:T(8,128)S(1)}, f32[256,128]{1,0:T(8,128)S(1)}) custom-call(s32[512]{0:T(512)S(1)} %pad_add_fusion.ids_ref, bf16[256,128,128]{2,1,0:T(8,128)(2,1)S(1)} %get-tuple-element.59.turned, f32[256,128]{1,0:T(8,128)S(1)} %pad_maximum_fusion.refs_0_, f32[256,128]{1,0:T(8,128)S(1)} %collective-permute-done.18.refs_1_, ...), custom_call_target="tpu_custom_call" | custom-call | flops 8388608 | bytes 8388608 | tf_op jit(solution)/shard_map/pallas_call | solution.py:414
  68.2 0.3 collective-permute-start.31
  68.5 1.2 %collective-permute-done.31 = f32[256,128]{1,0:T(8,128)S(1)} collective-permute-done((f32[256,128]{1,0:T(8,128)S(1)}, f32[256,128]{1,0:T(8,128)S(1)}, u32[]{:S(2)}, u32[]{:S(2)}) %collective-permute-start.31) | collective-permute-done | bytes 131104 | tf_op jit(solution)/shard_map/ppermute | solution.py:432
  69.7 1.4 %collective-permute-start.32 = (f32[256,128]{1,0:T(8,128)S(1)}, f32[256,128]{1,0:T(8,128)S(1)}, u32[]{:S(2)}, u32[]{:S(2)}) collective-permute-start(f32[256,128]{1,0:T(8,128)S(1)} %add.68), channel_id=1, source_target_pairs={{0,2},{1,3},{2,0},{3,1},{4,6},{5,7},{6,4},{7,5},{8,10},{9,11},{10,... | collective-permute-start | bytes 393224 | tf_op jit(solution)/shard_map/ppermute | solution.py:432
  71.0 4.3 %collective-permute-done.32 = f32[256,128]{1,0:T(8,128)S(1)} collective-permute-done((f32[256,128]{1,0:T(8,128)S(1)}, f32[256,128]{1,0:T(8,128)S(1)}, u32[]{:S(2)}, u32[]{:S(2)}) %collective-permute-start.32) | collective-permute-done | bytes 131104 | tf_op jit(solution)/shard_map/ppermute | solution.py:432
  75.4 1.3 %collective-permute-done.33.refs_1_ = f32[256,128]{1,0:T(8,128)S(1)} collective-permute-done((f32[256,128]{1,0:T(8,128)S(1)}, f32[256,128]{1,0:T(8,128)S(1)}, u32[]{:S(2)}, u32[]{:S(2)}) %collective-permute-start.33) | collective-permute-done | bytes 131104 | tf_op jit(solution)/shard_map/ppermute | solution.py:432
  76.8 2.5 %shard_map.120 = (f32[512,128]{1,0:T(8,128)S(1)}, f32[128,128]{1,0:T(8,128)S(1)}, f32[128,128]{1,0:T(8,128)S(1)}, f32[128,128]{1,0:T(8,128)S(1)}, f32[128,128]{1,0:T(8,128)S(1)}) custom-call(s32[512]{0:T(512)S(1)} %pad_add_fusion.ids_ref, bf16[256,128,128]{2,1,0:T(8,128)(2,1)S(1)} %get-tuple-element.55.blocks, f32[256,128]{1,0:T(8,128)S(1)} %add.69.refs_0_, ...), custom_call_target="tpu_custom_call" | custom-call | flops 8388608 | bytes 8388608 | tf_op jit(solution)/shard_map/pallas_call | solution.py:414
  79.3 1.3 %collective-permute-start.34 = (f32[128,128]{1,0:T(8,128)S(1)}, f32[128,128]{1,0:T(8,128)S(1)}, u32[]{:S(2)}, u32[]{:S(2)}) collective-permute-start(f32[128,128]{1,0:T(8,128)S(1)} %get-tuple-element.100), channel_id=1, source_target_pairs={{0,4},{4,0},{8,12},{12,8},{16,20},{20,16},{24,28},{28,24},{1,5},{5... | collective-permute-start | bytes 196616 | tf_op jit(solution)/shard_map/ppermute | solution.py:432
  80.6 1.0 collective-permute-start.35
  81.6 1.3 %collective-permute-start.36 = (f32[128,128]{1,0:T(8,128)S(1)}, f32[128,128]{1,0:T(8,128)S(1)}, u32[]{:S(2)}, u32[]{:S(2)}) collective-permute-start(f32[128,128]{1,0:T(8,128)S(1)} %get-tuple-element.102), channel_id=1, source_target_pairs={{0,12},{4,8},{8,4},{12,0},{16,28},{20,24},{24,20},{28,16},{1,13},{... | collective-permute-start | bytes 196616 | tf_op jit(solution)/shard_map/ppermute | solution.py:432
  82.9 0.8 collective-permute-done.34
  83.7 1.5 %collective-permute-done.35 = f32[128,128]{1,0:T(8,128)S(1)} collective-permute-done((f32[128,128]{1,0:T(8,128)S(1)}, f32[128,128]{1,0:T(8,128)S(1)}, u32[]{:S(2)}, u32[]{:S(2)}) %collective-permute-start.35) | collective-permute-done | bytes 65568 | tf_op jit(solution)/shard_map/ppermute | solution.py:432
  85.1 1.6 %collective-permute-done.36 = f32[128,128]{1,0:T(8,128)S(1)} collective-permute-done((f32[128,128]{1,0:T(8,128)S(1)}, f32[128,128]{1,0:T(8,128)S(1)}, u32[]{:S(2)}, u32[]{:S(2)}) %collective-permute-start.36) | collective-permute-done | bytes 65568 | tf_op jit(solution)/shard_map/ppermute | solution.py:432
  86.8 1.9 %collective-permute-start.37 = (f32[128,128]{1,0:T(8,128)S(1)}, f32[128,128]{1,0:T(8,128)S(1)}, u32[]{:S(2)}, u32[]{:S(2)}) collective-permute-start(f32[128,128]{1,0:T(8,128)S(1)} %add_add_fusion), channel_id=1, source_target_pairs={{0,16},{4,20},{8,24},{12,28},{16,0},{20,4},{24,8},{28,12},{1,17},{... | collective-permute-start | bytes 196616 | tf_op jit(solution)/shard_map/ppermute | solution.py:432
  88.7 4.1 %collective-permute-done.37 = f32[128,128]{1,0:T(8,128)S(1)} collective-permute-done((f32[128,128]{1,0:T(8,128)S(1)}, f32[128,128]{1,0:T(8,128)S(1)}, u32[]{:S(2)}, u32[]{:S(2)}) %collective-permute-start.37) | collective-permute-done | bytes 65568 | tf_op jit(solution)/shard_map/ppermute | solution.py:432
  92.8 0.6 collective-permute-start.40
  93.4 0.7 collective-permute-start.39
  94.1 2.3 %collective-permute-start.38 = (f32[128,128]{1,0:T(8,128)S(1)}, f32[128,128]{1,0:T(8,128)S(1)}, u32[]{:S(2)}, u32[]{:S(2)}) collective-permute-start(f32[128,128]{1,0:T(8,128)S(1)} %add.73.refs_0_), channel_id=1, source_target_pairs={{0,4},{4,0},{8,12},{12,8},{16,20},{20,16},{24,28},{28,24},{1,5},{5... | collective-permute-start | bytes 196616 | tf_op jit(solution)/shard_map/ppermute | solution.py:432
  96.4 1.7 %collective-permute-done.40.refs_3_ = f32[128,128]{1,0:T(8,128)S(1)} collective-permute-done((f32[128,128]{1,0:T(8,128)S(1)}, f32[128,128]{1,0:T(8,128)S(1)}, u32[]{:S(2)}, u32[]{:S(2)}) %collective-permute-start.40) | collective-permute-done | bytes 65568 | tf_op jit(solution)/shard_map/ppermute | solution.py:432
  98.0 0.7 collective-permute-done.38.refs_1_
  98.7 2.7 %shard_map.121 = (f32[512,128]{1,0:T(8,128)}, f32[256,128]{1,0:T(8,128)S(1)}, f32[256,128]{1,0:T(8,128)S(1)}) custom-call(s32[512]{0:T(512)S(1)} %pad_add_fusion.ids_ref, bf16[256,128,128]{2,1,0:T(8,128)(2,1)S(1)} %get-tuple-element.59.turned, f32[128,128]{1,0:T(8,128)S(1)} %add.73.refs_0_, f32[128,128]{1,0:T(8,128)S(1)} %collective-permute-done.38.refs_1_, ...), custom_call_target="tpu_custom_call" | custom-call | flops 8388608 | bytes 8388608 | tf_op jit(solution)/shard_map/pallas_call | solution.py:414
  101.5 1.3 %collective-permute-done.41 = f32[256,128]{1,0:T(8,128)S(1)} collective-permute-done((f32[256,128]{1,0:T(8,128)S(1)}, f32[256,128]{1,0:T(8,128)S(1)}, u32[]{:S(2)}, u32[]{:S(2)}) %collective-permute-start.41) | collective-permute-done | bytes 131104 | tf_op jit(solution)/shard_map/ppermute | solution.py:432
  102.9 1.8 %collective-permute-start.42 = (f32[256,128]{1,0:T(8,128)S(1)}, f32[256,128]{1,0:T(8,128)S(1)}, u32[]{:S(2)}, u32[]{:S(2)}) collective-permute-start(f32[256,128]{1,0:T(8,128)S(1)} %add.74), channel_id=1, source_target_pairs={{0,2},{1,3},{2,0},{3,1},{4,6},{5,7},{6,4},{7,5},{8,10},{9,11},{10,... | collective-permute-start | bytes 393224 | tf_op jit(solution)/shard_map/ppermute | solution.py:432
  104.6 3.9 %collective-permute-done.42 = f32[256,128]{1,0:T(8,128)S(1)} collective-permute-done((f32[256,128]{1,0:T(8,128)S(1)}, f32[256,128]{1,0:T(8,128)S(1)}, u32[]{:S(2)}, u32[]{:S(2)}) %collective-permute-start.42) | collective-permute-done | bytes 131104 | tf_op jit(solution)/shard_map/ppermute | solution.py:432
  108.6 1.3 %collective-permute-done.43.refs_1_ = f32[256,128]{1,0:T(8,128)S(1)} collective-permute-done((f32[256,128]{1,0:T(8,128)S(1)}, f32[256,128]{1,0:T(8,128)S(1)}, u32[]{:S(2)}, u32[]{:S(2)}) %collective-permute-start.43) | collective-permute-done | bytes 131104 | tf_op jit(solution)/shard_map/ppermute | solution.py:432
  109.9 0.9 shard_map.122
  (69 shorter events, 1.2 us)
Async XLA Ops:
  0.6 13.9 %copy-start.2 = (f32[65536]{0:T(1024)S(1)}, f32[65536]{0:T(1024)}, u32[]{:S(2)}) copy-start(f32[65536]{0:T(1024)} %param.19) | copy-start | bytes 786436
  7.1 4.0 %collective-permute-start = (f32[256,128]{1,0:T(8,128)S(1)}, f32[256,128]{1,0:T(8,128)S(1)}, u32[]{:S(2)}, u32[]{:S(2)}) collective-permute-start(f32[256,128]{1,0:T(8,128)S(1)} %get-tuple-element.57), channel_id=1, source_target_pairs={{0,1},{1,0},{2,3},{3,2},{4,5},{5,4},{6,7},{7,6},{8,9},{9,8},{10,11... | collective-permute-start | bytes 393224 | tf_op jit(solution)/shard_map/ppermute | solution.py:432
  7.6 10.0 %collective-permute-start.5 = (f32[128,128]{1,0:T(8,128)S(1)}, f32[128,128]{1,0:T(8,128)S(1)}, u32[]{:S(2)}, u32[]{:S(2)}) collective-permute-start(f32[128,128]{1,0:T(8,128)S(1)} %get-tuple-element.65), channel_id=1, source_target_pairs={{0,12},{4,8},{8,4},{12,0},{16,28},{20,24},{24,20},{28,16},{1,13},{... | collective-permute-start | bytes 196616 | tf_op jit(solution)/shard_map/ppermute | solution.py:432
  11.1 6.5 %collective-permute-start.3 = (f32[128,128]{1,0:T(8,128)S(1)}, f32[128,128]{1,0:T(8,128)S(1)}, u32[]{:S(2)}, u32[]{:S(2)}) collective-permute-start(f32[128,128]{1,0:T(8,128)S(1)} %get-tuple-element.63), channel_id=1, source_target_pairs={{0,4},{4,0},{8,12},{12,8},{16,20},{20,16},{24,28},{28,24},{1,5},{5... | collective-permute-start | bytes 196616 | tf_op jit(solution)/shard_map/ppermute | solution.py:432
  11.7 5.9 %collective-permute-start.4 = (f32[128,128]{1,0:T(8,128)S(1)}, f32[128,128]{1,0:T(8,128)S(1)}, u32[]{:S(2)}, u32[]{:S(2)}) collective-permute-start(f32[128,128]{1,0:T(8,128)S(1)} %get-tuple-element.64), channel_id=1, source_target_pairs={{0,8},{4,12},{8,0},{12,4},{16,24},{20,28},{24,16},{28,20},{1,9},{5... | collective-permute-start | bytes 196616 | tf_op jit(solution)/shard_map/ppermute | solution.py:432
  13.0 7.4 %collective-permute-start.1 = (f32[256,128]{1,0:T(8,128)S(1)}, f32[256,128]{1,0:T(8,128)S(1)}, u32[]{:S(2)}, u32[]{:S(2)}) collective-permute-start(f32[256,128]{1,0:T(8,128)S(1)} %max.36), channel_id=1, source_target_pairs={{0,2},{1,3},{2,0},{3,1},{4,6},{5,7},{6,4},{7,5},{8,10},{9,11},{10,... | collective-permute-start | bytes 393224 | tf_op jit(solution)/shard_map/ppermute | solution.py:432
  17.7 6.3 %collective-permute-start.6 = (f32[128,128]{1,0:T(8,128)S(1)}, f32[128,128]{1,0:T(8,128)S(1)}, u32[]{:S(2)}, u32[]{:S(2)}) collective-permute-start(f32[128,128]{1,0:T(8,128)S(1)} %maximum_maximum_fusion.1), channel_id=1, source_target_pairs={{0,16},{4,20},{8,24},{12,28},{16,0},{20,4},{24,8},{28,12},{1,17},{... | collective-permute-start | bytes 196616 | tf_op jit(solution)/shard_map/ppermute | solution.py:432
  20.4 5.3 %collective-permute-start.14 = (f32[128,128]{1,0:T(8,128)S(1)}, f32[128,128]{1,0:T(8,128)S(1)}, u32[]{:S(2)}, u32[]{:S(2)}) collective-permute-start(f32[128,128]{1,0:T(8,128)S(1)} %get-tuple-element.82), channel_id=1, source_target_pairs={{0,4},{4,0},{8,12},{12,8},{16,20},{20,16},{24,28},{28,24},{1,5},{5... | collective-permute-start | bytes 196616 | tf_op jit(solution)/shard_map/ppermute | solution.py:432
  21.1 5.0 %collective-permute-start.15 = (f32[128,128]{1,0:T(8,128)S(1)}, f32[128,128]{1,0:T(8,128)S(1)}, u32[]{:S(2)}, u32[]{:S(2)}) collective-permute-start(f32[128,128]{1,0:T(8,128)S(1)} %get-tuple-element.83), channel_id=1, source_target_pairs={{0,8},{4,12},{8,0},{12,4},{16,24},{20,28},{24,16},{28,20},{1,9},{5... | collective-permute-start | bytes 196616 | tf_op jit(solution)/shard_map/ppermute | solution.py:432
  22.7 5.2 %collective-permute-start.16 = (f32[128,128]{1,0:T(8,128)S(1)}, f32[128,128]{1,0:T(8,128)S(1)}, u32[]{:S(2)}, u32[]{:S(2)}) collective-permute-start(f32[128,128]{1,0:T(8,128)S(1)} %get-tuple-element.84), channel_id=1, source_target_pairs={{0,12},{4,8},{8,4},{12,0},{16,28},{20,24},{24,20},{28,16},{1,13},{... | collective-permute-start | bytes 196616 | tf_op jit(solution)/shard_map/ppermute | solution.py:432
  24.0 3.9 %collective-permute-start.2 = (f32[256,128]{1,0:T(8,128)S(1)}, f32[256,128]{1,0:T(8,128)S(1)}, u32[]{:S(2)}, u32[]{:S(2)}) collective-permute-start(f32[256,128]{1,0:T(8,128)S(1)} %max.37.refs_0_), channel_id=1, source_target_pairs={{0,1},{1,0},{2,3},{3,2},{4,5},{5,4},{6,7},{7,6},{8,9},{9,8},{10,11... | collective-permute-start | bytes 393224 | tf_op jit(solution)/shard_map/ppermute | solution.py:432
  24.0 8.0 %collective-permute-start.9 = (f32[128,128]{1,0:T(8,128)S(1)}, f32[128,128]{1,0:T(8,128)S(1)}, u32[]{:S(2)}, u32[]{:S(2)}) collective-permute-start(f32[128,128]{1,0:T(8,128)S(1)} %max.41.refs_0_), channel_id=1, source_target_pairs={{0,12},{4,8},{8,4},{12,0},{16,28},{20,24},{24,20},{28,16},{1,13},{... | collective-permute-start | bytes 196616 | tf_op jit(solution)/shard_map/ppermute | solution.py:432
  25.7 6.3 %collective-permute-start.8 = (f32[128,128]{1,0:T(8,128)S(1)}, f32[128,128]{1,0:T(8,128)S(1)}, u32[]{:S(2)}, u32[]{:S(2)}) collective-permute-start(f32[128,128]{1,0:T(8,128)S(1)} %max.41.refs_0_), channel_id=1, source_target_pairs={{0,8},{4,12},{8,0},{12,4},{16,24},{20,28},{24,16},{28,20},{1,9},{5... | collective-permute-start | bytes 196616 | tf_op jit(solution)/shard_map/ppermute | solution.py:432
  26.2 5.9 %collective-permute-start.7 = (f32[128,128]{1,0:T(8,128)S(1)}, f32[128,128]{1,0:T(8,128)S(1)}, u32[]{:S(2)}, u32[]{:S(2)}) collective-permute-start(f32[128,128]{1,0:T(8,128)S(1)} %max.41.refs_0_), channel_id=1, source_target_pairs={{0,4},{4,0},{8,12},{12,8},{16,20},{20,16},{24,28},{28,24},{1,5},{5... | collective-permute-start | bytes 196616 | tf_op jit(solution)/shard_map/ppermute | solution.py:432
  32.0 21.4 %copy-start = (f32[65536]{0:T(1024)S(1)}, f32[65536]{0:T(1024)}, u32[]{:S(2)}) copy-start(f32[65536]{0:T(1024)} %param.14) | copy-start | bytes 786436
  32.0 29.7 %copy-start.1 = (f32[65536]{0:T(1024)S(1)}, f32[65536]{0:T(1024)}, u32[]{:S(2)}) copy-start(f32[65536]{0:T(1024)} %param.13) | copy-start | bytes 786436
  32.0 33.5 %copy-start.3 = (f32[65536]{0:T(1024)S(1)}, f32[65536]{0:T(1024)}, u32[]{:S(2)}) copy-start(f32[65536]{0:T(1024)} %param.15) | copy-start | bytes 786436
  32.0 33.5 %copy-start.4 = (f32[65536]{0:T(1024)S(1)}, f32[65536]{0:T(1024)}, u32[]{:S(2)}) copy-start(f32[65536]{0:T(1024)} %param.16) | copy-start | bytes 786436
  32.0 33.5 %copy-start.5 = (s32[65536]{0:T(1024)S(1)}, s32[65536]{0:T(1024)}, u32[]{:S(2)}) copy-start(s32[65536]{0:T(1024)} %param.17) | copy-start | bytes 786436
  32.0 33.5 %copy-start.6 = (f32[65536]{0:T(1024)S(1)}, f32[65536]{0:T(1024)}, u32[]{:S(2)}) copy-start(f32[65536]{0:T(1024)} %param.18) | copy-start | bytes 786436
  32.1 9.5 %collective-permute-start.10 = (f32[128,128]{1,0:T(8,128)S(1)}, f32[128,128]{1,0:T(8,128)S(1)}, u32[]{:S(2)}, u32[]{:S(2)}) collective-permute-start(f32[128,128]{1,0:T(8,128)S(1)} %get-tuple-element.78), channel_id=1, source_target_pairs={{0,4},{4,0},{8,12},{12,8},{16,20},{20,16},{24,28},{28,24},{1,5},{5... | collective-permute-start | bytes 196616 | tf_op jit(solution)/shard_map/ppermute | solution.py:432
  32.4 9.1 %collective-permute-start.17 = (f32[128,128]{1,0:T(8,128)S(1)}, f32[128,128]{1,0:T(8,128)S(1)}, u32[]{:S(2)}, u32[]{:S(2)}) collective-permute-start(f32[128,128]{1,0:T(8,128)S(1)} %add_add_fusion.1), channel_id=1, source_target_pairs={{0,16},{4,20},{8,24},{12,28},{16,0},{20,4},{24,8},{28,12},{1,17},{... | collective-permute-start | bytes 196616 | tf_op jit(solution)/shard_map/ppermute | solution.py:432
  34.6 6.9 %collective-permute-start.11 = (f32[128,128]{1,0:T(8,128)S(1)}, f32[128,128]{1,0:T(8,128)S(1)}, u32[]{:S(2)}, u32[]{:S(2)}) collective-permute-start(f32[128,128]{1,0:T(8,128)S(1)} %get-tuple-element.79), channel_id=1, source_target_pairs={{0,8},{4,12},{8,0},{12,4},{16,24},{20,28},{24,16},{28,20},{1,9},{5... | collective-permute-start | bytes 196616 | tf_op jit(solution)/shard_map/ppermute | solution.py:432
  36.3 5.3 %collective-permute-start.12 = (f32[128,128]{1,0:T(8,128)S(1)}, f32[128,128]{1,0:T(8,128)S(1)}, u32[]{:S(2)}, u32[]{:S(2)}) collective-permute-start(f32[128,128]{1,0:T(8,128)S(1)} %get-tuple-element.80), channel_id=1, source_target_pairs={{0,12},{4,8},{8,4},{12,0},{16,28},{20,24},{24,20},{28,16},{1,13},{... | collective-permute-start | bytes 196616 | tf_op jit(solution)/shard_map/ppermute | solution.py:432
  41.6 1.4 %collective-permute-start.21 = (f32[256,128]{1,0:T(8,128)S(1)}, f32[256,128]{1,0:T(8,128)S(1)}, u32[]{:S(2)}, u32[]{:S(2)}) collective-permute-start(f32[256,128]{1,0:T(8,128)S(1)} %get-tuple-element.92), channel_id=1, source_target_pairs={{0,1},{1,0},{2,3},{3,2},{4,5},{5,4},{6,7},{7,6},{8,9},{9,8},{10,11... | collective-permute-start | bytes 393224 | tf_op jit(solution)/shard_map/ppermute | solution.py:432
  43.1 6.6 %collective-permute-start.22 = (f32[256,128]{1,0:T(8,128)S(1)}, f32[256,128]{1,0:T(8,128)S(1)}, u32[]{:S(2)}, u32[]{:S(2)}) collective-permute-start(f32[256,128]{1,0:T(8,128)S(1)} %max.46), channel_id=1, source_target_pairs={{0,2},{1,3},{2,0},{3,1},{4,6},{5,7},{6,4},{7,5},{8,10},{9,11},{10,... | collective-permute-start | bytes 393224 | tf_op jit(solution)/shard_map/ppermute | solution.py:432
  43.4 6.2 %collective-permute-start.13 = (f32[128,128]{1,0:T(8,128)S(1)}, f32[128,128]{1,0:T(8,128)S(1)}, u32[]{:S(2)}, u32[]{:S(2)}) collective-permute-start(f32[128,128]{1,0:T(8,128)S(1)} %maximum_maximum_fusion), channel_id=1, source_target_pairs={{0,16},{4,20},{8,24},{12,28},{16,0},{20,4},{24,8},{28,12},{1,17},{... | collective-permute-start | bytes 196616 | tf_op jit(solution)/shard_map/ppermute | solution.py:432
  49.7 3.7 %collective-permute-start.23 = (f32[256,128]{1,0:T(8,128)S(1)}, f32[256,128]{1,0:T(8,128)S(1)}, u32[]{:S(2)}, u32[]{:S(2)}) collective-permute-start(f32[256,128]{1,0:T(8,128)S(1)} %max.47.near), channel_id=1, source_target_pairs={{0,1},{1,0},{2,3},{3,2},{4,5},{5,4},{6,7},{7,6},{8,9},{9,8},{10,11... | collective-permute-start | bytes 393224 | tf_op jit(solution)/shard_map/ppermute | solution.py:432
  49.8 10.5 %collective-permute-start.20 = (f32[256,128]{1,0:T(8,128)S(1)}, f32[256,128]{1,0:T(8,128)S(1)}, u32[]{:S(2)}, u32[]{:S(2)}) collective-permute-start(f32[256,128]{1,0:T(8,128)S(1)} %pad_maximum_fusion.refs_0_), channel_id=1, source_target_pairs={{0,12},{4,8},{8,4},{12,0},{16,28},{20,24},{24,20},{28,16},{1,13},{... | collective-permute-start | bytes 393224 | tf_op jit(solution)/shard_map/ppermute | solution.py:432
  50.6 11.0 %collective-permute-start.19 = (f32[256,128]{1,0:T(8,128)S(1)}, f32[256,128]{1,0:T(8,128)S(1)}, u32[]{:S(2)}, u32[]{:S(2)}) collective-permute-start(f32[256,128]{1,0:T(8,128)S(1)} %pad_maximum_fusion.refs_0_), channel_id=1, source_target_pairs={{0,8},{4,12},{8,0},{12,4},{16,24},{20,28},{24,16},{28,20},{1,9},{5... | collective-permute-start | bytes 393224 | tf_op jit(solution)/shard_map/ppermute | solution.py:432
  52.4 9.2 %collective-permute-start.18 = (f32[256,128]{1,0:T(8,128)S(1)}, f32[256,128]{1,0:T(8,128)S(1)}, u32[]{:S(2)}, u32[]{:S(2)}) collective-permute-start(f32[256,128]{1,0:T(8,128)S(1)} %pad_maximum_fusion.refs_0_), channel_id=1, source_target_pairs={{0,4},{4,0},{8,12},{12,8},{16,20},{20,16},{24,28},{28,24},{1,5},{5... | collective-permute-start | bytes 393224 | tf_op jit(solution)/shard_map/ppermute | solution.py:432
  53.4 4.7 %collective-permute-start.24 = (f32[8,128]{1,0:T(8,128)S(1)}, f32[8,128]{1,0:T(8,128)S(1)}, u32[]{:S(2)}, u32[]{:S(2)}) collective-permute-start(f32[8,128]{1,0:T(8,128)S(1)} %get-tuple-element.94), channel_id=1, source_target_pairs={{0,16},{4,20},{8,24},{12,28},{16,0},{20,4},{24,8},{28,12},{1,17},{... | collective-permute-start | bytes 12296 | tf_op jit(solution)/shard_map/ppermute | solution.py:432
  58.1 3.6 %collective-permute-start.25 = (f32[8,128]{1,0:T(8,128)S(1)}, f32[8,128]{1,0:T(8,128)S(1)}, u32[]{:S(2)}, u32[]{:S(2)}) collective-permute-start(f32[8,128]{1,0:T(8,128)S(1)} %add.61), channel_id=1, source_target_pairs={{0,4},{4,0},{8,12},{12,8},{16,20},{20,16},{24,28},{28,24},{1,5},{5... | collective-permute-start | bytes 12296 | tf_op jit(solution)/shard_map/ppermute | solution.py:432
  59.2 4.5 %collective-permute-start.30 = (f32[8,128]{1,0:T(8,128)S(1)}, f32[8,128]{1,0:T(8,128)S(1)}, u32[]{:S(2)}, u32[]{:S(2)}) collective-permute-start(f32[8,128]{1,0:T(8,128)S(1)} %add.61), channel_id=1, source_target_pairs={{0,12},{4,8},{8,4},{12,0},{16,28},{20,24},{24,20},{28,16},{1,13},{... | collective-permute-start | bytes 12296 | tf_op jit(solution)/shard_map/ppermute | solution.py:432
  60.3 3.6 %collective-permute-start.29 = (f32[8,128]{1,0:T(8,128)S(1)}, f32[8,128]{1,0:T(8,128)S(1)}, u32[]{:S(2)}, u32[]{:S(2)}) collective-permute-start(f32[8,128]{1,0:T(8,128)S(1)} %add.61), channel_id=1, source_target_pairs={{0,8},{4,12},{8,0},{12,4},{16,24},{20,28},{24,16},{28,20},{1,9},{5... | collective-permute-start | bytes 12296 | tf_op jit(solution)/shard_map/ppermute | solution.py:432
  61.7 3.1 %collective-permute-start.28 = (f32[8,128]{1,0:T(8,128)S(1)}, f32[8,128]{1,0:T(8,128)S(1)}, u32[]{:S(2)}, u32[]{:S(2)}) collective-permute-start(f32[8,128]{1,0:T(8,128)S(1)} %get-tuple-element.95), channel_id=1, source_target_pairs={{0,3},{1,2},{2,1},{3,0},{4,7},{5,6},{6,5},{7,4},{8,11},{9,10},{10,... | collective-permute-start | bytes 12296 | tf_op jit(solution)/shard_map/ppermute | solution.py:432
  61.8 3.7 %collective-permute-start.27 = (f32[8,128]{1,0:T(8,128)S(1)}, f32[8,128]{1,0:T(8,128)S(1)}, u32[]{:S(2)}, u32[]{:S(2)}) collective-permute-start(f32[8,128]{1,0:T(8,128)S(1)} %get-tuple-element.95), channel_id=1, source_target_pairs={{0,2},{1,3},{2,0},{3,1},{4,6},{5,7},{6,4},{7,5},{8,10},{9,11},{10,... | collective-permute-start | bytes 12296 | tf_op jit(solution)/shard_map/ppermute | solution.py:432
  63.2 2.2 %collective-permute-start.26 = (f32[8,128]{1,0:T(8,128)S(1)}, f32[8,128]{1,0:T(8,128)S(1)}, u32[]{:S(2)}, u32[]{:S(2)}) collective-permute-start(f32[8,128]{1,0:T(8,128)S(1)} %get-tuple-element.95), channel_id=1, source_target_pairs={{0,1},{1,0},{2,3},{3,2},{4,5},{5,4},{6,7},{7,6},{8,9},{9,8},{10,11... | collective-permute-start | bytes 12296 | tf_op jit(solution)/shard_map/ppermute | solution.py:432
  68.2 1.4 %collective-permute-start.31 = (f32[256,128]{1,0:T(8,128)S(1)}, f32[256,128]{1,0:T(8,128)S(1)}, u32[]{:S(2)}, u32[]{:S(2)}) collective-permute-start(f32[256,128]{1,0:T(8,128)S(1)} %get-tuple-element.97), channel_id=1, source_target_pairs={{0,1},{1,0},{2,3},{3,2},{4,5},{5,4},{6,7},{7,6},{8,9},{9,8},{10,11... | collective-permute-start | bytes 393224 | tf_op jit(solution)/shard_map/ppermute | solution.py:432
  69.7 5.7 %collective-permute-start.32 = (f32[256,128]{1,0:T(8,128)S(1)}, f32[256,128]{1,0:T(8,128)S(1)}, u32[]{:S(2)}, u32[]{:S(2)}) collective-permute-start(f32[256,128]{1,0:T(8,128)S(1)} %add.68), channel_id=1, source_target_pairs={{0,2},{1,3},{2,0},{3,1},{4,6},{5,7},{6,4},{7,5},{8,10},{9,11},{10,... | collective-permute-start | bytes 393224 | tf_op jit(solution)/shard_map/ppermute | solution.py:432
  75.4 1.4 %collective-permute-start.33 = (f32[256,128]{1,0:T(8,128)S(1)}, f32[256,128]{1,0:T(8,128)S(1)}, u32[]{:S(2)}, u32[]{:S(2)}) collective-permute-start(f32[256,128]{1,0:T(8,128)S(1)} %add.69.refs_0_), channel_id=1, source_target_pairs={{0,1},{1,0},{2,3},{3,2},{4,5},{5,4},{6,7},{7,6},{8,9},{9,8},{10,11... | collective-permute-start | bytes 393224 | tf_op jit(solution)/shard_map/ppermute | solution.py:432
  79.3 4.3 %collective-permute-start.34 = (f32[128,128]{1,0:T(8,128)S(1)}, f32[128,128]{1,0:T(8,128)S(1)}, u32[]{:S(2)}, u32[]{:S(2)}) collective-permute-start(f32[128,128]{1,0:T(8,128)S(1)} %get-tuple-element.100), channel_id=1, source_target_pairs={{0,4},{4,0},{8,12},{12,8},{16,20},{20,16},{24,28},{28,24},{1,5},{5... | collective-permute-start | bytes 196616 | tf_op jit(solution)/shard_map/ppermute | solution.py:432
  80.6 4.6 %collective-permute-start.35 = (f32[128,128]{1,0:T(8,128)S(1)}, f32[128,128]{1,0:T(8,128)S(1)}, u32[]{:S(2)}, u32[]{:S(2)}) collective-permute-start(f32[128,128]{1,0:T(8,128)S(1)} %get-tuple-element.101), channel_id=1, source_target_pairs={{0,8},{4,12},{8,0},{12,4},{16,24},{20,28},{24,16},{28,20},{1,9},{5... | collective-permute-start | bytes 196616 | tf_op jit(solution)/shard_map/ppermute | solution.py:432
  81.6 5.2 %collective-permute-start.36 = (f32[128,128]{1,0:T(8,128)S(1)}, f32[128,128]{1,0:T(8,128)S(1)}, u32[]{:S(2)}, u32[]{:S(2)}) collective-permute-start(f32[128,128]{1,0:T(8,128)S(1)} %get-tuple-element.102), channel_id=1, source_target_pairs={{0,12},{4,8},{8,4},{12,0},{16,28},{20,24},{24,20},{28,16},{1,13},{... | collective-permute-start | bytes 196616 | tf_op jit(solution)/shard_map/ppermute | solution.py:432
  86.8 6.0 %collective-permute-start.37 = (f32[128,128]{1,0:T(8,128)S(1)}, f32[128,128]{1,0:T(8,128)S(1)}, u32[]{:S(2)}, u32[]{:S(2)}) collective-permute-start(f32[128,128]{1,0:T(8,128)S(1)} %add_add_fusion), channel_id=1, source_target_pairs={{0,16},{4,20},{8,24},{12,28},{16,0},{20,4},{24,8},{28,12},{1,17},{... | collective-permute-start | bytes 196616 | tf_op jit(solution)/shard_map/ppermute | solution.py:432
  92.8 5.2 %collective-permute-start.40 = (f32[128,128]{1,0:T(8,128)S(1)}, f32[128,128]{1,0:T(8,128)S(1)}, u32[]{:S(2)}, u32[]{:S(2)}) collective-permute-start(f32[128,128]{1,0:T(8,128)S(1)} %add.73.refs_0_), channel_id=1, source_target_pairs={{0,12},{4,8},{8,4},{12,0},{16,28},{20,24},{24,20},{28,16},{1,13},{... | collective-permute-start | bytes 196616 | tf_op jit(solution)/shard_map/ppermute | solution.py:432
  93.4 4.7 %collective-permute-start.39 = (f32[128,128]{1,0:T(8,128)S(1)}, f32[128,128]{1,0:T(8,128)S(1)}, u32[]{:S(2)}, u32[]{:S(2)}) collective-permute-start(f32[128,128]{1,0:T(8,128)S(1)} %add.73.refs_0_), channel_id=1, source_target_pairs={{0,8},{4,12},{8,0},{12,4},{16,24},{20,28},{24,16},{28,20},{1,9},{5... | collective-permute-start | bytes 196616 | tf_op jit(solution)/shard_map/ppermute | solution.py:432
  94.1 4.6 %collective-permute-start.38 = (f32[128,128]{1,0:T(8,128)S(1)}, f32[128,128]{1,0:T(8,128)S(1)}, u32[]{:S(2)}, u32[]{:S(2)}) collective-permute-start(f32[128,128]{1,0:T(8,128)S(1)} %add.73.refs_0_), channel_id=1, source_target_pairs={{0,4},{4,0},{8,12},{12,8},{16,20},{20,16},{24,28},{28,24},{1,5},{5... | collective-permute-start | bytes 196616 | tf_op jit(solution)/shard_map/ppermute | solution.py:432
  101.4 1.4 %collective-permute-start.41 = (f32[256,128]{1,0:T(8,128)S(1)}, f32[256,128]{1,0:T(8,128)S(1)}, u32[]{:S(2)}, u32[]{:S(2)}) collective-permute-start(f32[256,128]{1,0:T(8,128)S(1)} %get-tuple-element.106), channel_id=1, source_target_pairs={{0,1},{1,0},{2,3},{3,2},{4,5},{5,4},{6,7},{7,6},{8,9},{9,8},{10,11... | collective-permute-start | bytes 393224 | tf_op jit(solution)/shard_map/ppermute | solution.py:432
  102.9 5.6 %collective-permute-start.42 = (f32[256,128]{1,0:T(8,128)S(1)}, f32[256,128]{1,0:T(8,128)S(1)}, u32[]{:S(2)}, u32[]{:S(2)}) collective-permute-start(f32[256,128]{1,0:T(8,128)S(1)} %add.74), channel_id=1, source_target_pairs={{0,2},{1,3},{2,0},{3,1},{4,6},{5,7},{6,4},{7,5},{8,10},{9,11},{10,... | collective-permute-start | bytes 393224 | tf_op jit(solution)/shard_map/ppermute | solution.py:432
  108.5 1.4 %collective-permute-start.43 = (f32[256,128]{1,0:T(8,128)S(1)}, f32[256,128]{1,0:T(8,128)S(1)}, u32[]{:S(2)}, u32[]{:S(2)}) collective-permute-start(f32[256,128]{1,0:T(8,128)S(1)} %add.75.refs_0_), channel_id=1, source_target_pairs={{0,1},{1,0},{2,3},{3,2},{4,5},{5,4},{6,7},{7,6},{8,9},{9,8},{10,11... | collective-permute-start | bytes 393224 | tf_op jit(solution)/shard_map/ppermute | solution.py:432
